TPU v7x, 256 devices: a whole 4x4x8 slice. The times are simulated.
256 devices in a mesh: ctx: 32 (over y, x, core), head: 8 (over z).
Axes of the slice: x: 4, y: 4, z: 8, core: 2. Of those that a mesh axis runs over, the one named last changes fastest.
Arguments:
- queries: bfloat16 [16384, 4096], P('ctx', 'head'), may hold values from -6 to 6
- keys: bfloat16 [16384, 4096], P('ctx', 'head'), may hold values from -6 to 6
- values: bfloat16 [16384, 4096], P('ctx', 'head'), may hold values from -6 to 6
- log_decay: float32 [32, 16384], P('head', 'ctx'), may hold values from -2 to 0
- level_pick: int32 [32, 16384], P('head', 'ctx'), may hold values from 0 to 15
- level_table: float32 [32, 8, 16], P('head'), may hold values from 0.2 to 2
- out_weight: bfloat16 [4096, 8192], P('head', 'ctx'), may hold values from -0.1875 to 0.1875
Outputs:
- layer_out: bfloat16 [16384, 8192], P('ctx', 'head')
All inputs are finite; a program needn't handle non-finite values.
Results may differ from a plain program's by a relative error of at most 0.024.
Values may be sent and summed in bfloat16 or wider, within the bound.
A program may use at most 128 MiB of HBM per device.

v0:
```python
import jax
import jax.numpy as jnp
import numpy as np
from jax import lax
from jax.sharding import PartitionSpec as P

HD = 128
BLOCK = 128


def local(queries, keys, values, log_decay, level_pick, level_table, out_weight):
    token_count = queries.shape[0]
    head_count = log_decay.shape[0]
    block_count = token_count // BLOCK
    level_count = level_table.shape[1]
    table_size = level_table.shape[2]
    query_blocks = queries.reshape(block_count, BLOCK, head_count, HD)
    key_blocks = keys.reshape(block_count, BLOCK, head_count, HD)
    value_blocks = values.reshape(block_count, BLOCK, head_count, HD)
    within = jnp.cumsum(log_decay.reshape(head_count, block_count, BLOCK), axis=2)
    block_decay = within[:, :, -1]
    block_end = jnp.cumsum(block_decay, axis=1)
    block_start = block_end - block_decay
    one_hot = (
        level_pick[:, None, :] == lax.broadcasted_iota(jnp.int32, (1, table_size, 1), 1)
    ).astype(jnp.float32)
    level_weight = jnp.einsum("hlk,hkt->hlt", level_table, one_hot, precision=lax.Precision.HIGHEST)
    level_weight = level_weight.reshape(head_count, level_count, block_count, BLOCK)
    scores = jnp.einsum(
        "cthd,cshd->hcts", query_blocks, key_blocks, preferred_element_type=jnp.float32
    )
    rows = lax.broadcasted_iota(jnp.int32, (BLOCK, BLOCK), 0)
    cols = lax.broadcasted_iota(jnp.int32, (BLOCK, BLOCK), 1)
    causal = rows >= cols
    log_gaps = within[:, :, :, None] - within[:, :, None, :]
    decays = jnp.where(causal, jnp.exp(jnp.where(causal, log_gaps, 0.0)), 0.0)
    weights = (level_weight[:, 0, :, :, None] * decays * scores).astype(jnp.bfloat16)
    local_out = jnp.einsum(
        "hcts,cshd->hctd", weights, value_blocks, preferred_element_type=jnp.float32
    )
    scaled = jnp.exp(block_decay[:, :, None] - within)
    block_keys = (key_blocks * jnp.transpose(scaled, (1, 2, 0))[:, :, :, None]).astype(jnp.bfloat16)
    states = jnp.einsum(
        "cshd,cshe->hcde", block_keys, value_blocks, preferred_element_type=jnp.float32
    )
    level_list = []
    dev_bits = block_count.bit_length() - 1
    numbers = np.arange(block_count)
    for level in range(dev_bits):
        upper_end = numbers >> level << level
        bit_set = numbers >> level & 1 == 1
        inside = (
            bit_set[:, None]
            & (numbers[None, :] >= (upper_end - (1 << level))[:, None])
            & (numbers[None, :] < upper_end[:, None])
        )
        factors = jnp.where(
            jnp.asarray(inside)[None],
            jnp.exp(jnp.minimum(block_start[:, :, None] - block_end[:, None, :], 0.0)),
            0.0,
        )
        level_list.append(
            jnp.einsum("hcm,hmde->hcde", factors, states, precision=lax.Precision.HIGHEST)
        )
    summary = jnp.einsum(
        "hm,hmde->hde",
        jnp.exp(block_end[:, -1:] - block_end),
        states,
        precision=lax.Precision.HIGHEST,
    )
    total_decay = block_end[:, -1]
    ctx_bits = lax.axis_size("ctx").bit_length() - 1
    my_index = lax.axis_index("ctx")
    remote_list = []
    all_decay = lax.all_gather(total_decay[None, :], "ctx", axis=0, tiled=True)
    running_end = jnp.cumsum(all_decay, axis=0)
    own_start = lax.dynamic_index_in_dim(running_end - all_decay, my_index, 0, keepdims=False)
    bit_ids = jnp.arange(ctx_bits, dtype=jnp.int32)
    upper_dev = my_index >> bit_ids << bit_ids
    lower_dev = upper_dev - (1 << bit_ids)
    dev_set = my_index >> bit_ids & 1 == 1
    initial = jnp.zeros((ctx_bits, head_count, HD, HD), jnp.float32)
    block_rows = lax.all_gather(
        summary[None].astype(jnp.bfloat16), "ctx", axis=0, tiled=True
    ).astype(jnp.float32)
    row_count = block_rows.shape[0]
    device_ids = jnp.arange(row_count, dtype=jnp.int32)
    member = (
        dev_set[:, None]
        & (device_ids[None, :] >= lower_dev[:, None])
        & (device_ids[None, :] < upper_dev[:, None])
    )
    factors = jnp.where(
        member[:, :, None],
        jnp.exp(jnp.minimum(own_start[None, None, :] - running_end[None, :, :], 0.0)),
        0.0,
    )
    remote = initial + jnp.einsum(
        "jnh,nhde->jhde", factors, block_rows, precision=lax.Precision.HIGHEST
    )
    for level in range(ctx_bits):
        remote_list.append(remote[level])
    for remote_state in remote_list:
        level_list.append(jnp.exp(block_start)[:, :, None, None] * remote_state[:, None, :, :])
    level_total = len(level_list)
    stacked = jnp.concatenate(level_list, axis=2).astype(jnp.bfloat16)
    query_heads = jnp.transpose(query_blocks, (2, 0, 1, 3))
    level_queries = (
        level_weight[:, 1:, :, :, None]
        * jnp.exp(within)[:, None, :, :, None]
        * query_heads[:, None]
    )
    level_queries = (
        jnp.transpose(level_queries, (0, 2, 3, 1, 4))
        .reshape(head_count, block_count, BLOCK, level_total * HD)
        .astype(jnp.bfloat16)
    )
    readout = jnp.einsum(
        "hctk,hcke->hcte", level_queries, stacked, preferred_element_type=jnp.float32
    )
    mixture = local_out + readout
    normed = (
        mixture * lax.rsqrt(jnp.mean(mixture * mixture, axis=-1, keepdims=True) + 1e-06)
    ).astype(jnp.bfloat16)
    flattened = jnp.transpose(normed, (1, 2, 0, 3)).reshape(token_count, head_count * HD)
    projected = jnp.dot(
        flattened,
        lax.all_gather(out_weight, "ctx", axis=1, tiled=True),
        preferred_element_type=jnp.float32,
    )
    final_output = lax.psum_scatter(
        projected.astype(jnp.bfloat16), "head", scatter_dimension=1, tiled=True
    )
    return final_output


def solution(mesh):
    in_specs = (
        P("ctx", "head"),
        P("ctx", "head"),
        P("ctx", "head"),
        P("head", "ctx"),
        P("head", "ctx"),
        P("head", None, None),
        P("head", "ctx"),
    )
    out_specs = P("ctx", "head")
    return jax.shard_map(local, mesh=mesh, in_specs=in_specs, out_specs=out_specs, check_vma=False)
```

profile of v0, /device:TPU:1, one launch (start us, length us, event | category | flops | bytes accessed | tf_op | source)
XLA Modules:
  0.0 248.4 jit_solution(14025969505748591224)
XLA Ops:
  6.5 0.7 reshape.165
  7.3 1.2 reduce_window_sum.37
  8.5 0.2 slice_reduce_fusion
  8.6 0.2 reduce_window_sum.38
  8.8 0.2 slice_reduce_fusion.1
  9.0 0.1 subtract_exponential_fusion.1
  9.1 0.1 fusion.42
  9.2 1.2 reshape.167
  10.4 0.4 copy.41
  10.8 1.2 reshape.168
  12.0 0.3 fusion.20
  12.3 2.4 fusion.17
  14.7 0.7 convert_element_type.45
  15.4 0.0 all-gather.7.cloned.1.call-update
  15.4 0.0 all-gather.5.cloned.1.call-start
  15.4 0.7 all-gather.5.cloned.1.call-update
  16.1 0.0 reduce-scatter.2.cloned.1.call-start
  16.2 0.6 dynamic-slice
  17.5 0.2 dynamic-update-slice
  17.7 65.7 %all-reduce = f32[128]{0:T(128)S(1)} all-reduce(f32[128]{0:T(128)S(1)} %dynamic-update-slice), channel_id=3, replica_groups=mesh['ctx'=32,'head'=8] {'ctx'}, use_global_device_ids=true, to_apply=%add | all-reduce | flops 128 | bytes 1024
  83.4 0.1 reshape.171
  83.5 0.1 reduce_window_sum.41
  83.6 0.1 copy.45
  83.7 0.1 copy.40
  83.8 0.1 reshape.166
  83.9 0.4 copy.39
  84.3 0.2 convolution_bitcast_fusion
  84.6 0.2 subtract_reduce_fusion
  84.7 0.1 fusion.55
  84.8 0.1 convert_bitcast_fusion
  84.9 3.2 %fusion.7 = bf16[4,4,896,128]{3,1,2,0:T(4,128)(2,1)} fusion(f32[4,4,128,128]{3,2,1,0:T(8,128)S(1)} %fusion.20, f32[4,4]{1,0:T(4,128)S(1)} %reduce_window_sum.38, f32[4,4]{1,0:T(4,128)S(1)} %subtract_reduce_fusion, pred[4,4]{1,0:T(4,128)(4,1)S(1)} %copy-done.7), kind=kOutput, calls=%fused_computation.11 | convolution fusion | flops 12845247 | bytes 1573008 | tf_op jit(solution)/shard_map/hcm,hmde->hcde/dot_general | solution.py:63
  88.1 3.2 %fusion.8 = bf16[4,4,896,128]{3,1,2,0:T(4,128)(2,1)} fusion(bf16[4,4,896,128]{3,1,2,0:T(4,128)(2,1)} %fusion.7, f32[4,4,128,128]{3,2,1,0:T(8,128)S(1)} %fusion.20, f32[4,4]{1,0:T(4,128)S(1)} %reduce_window_sum.38, f32[4,4]{1,0:T(4,128)S(1)} %subtract_reduce_fusion, pred[4,4]{1,0:T(4,128)(4,1)S(1)} %copy-done.5), kind=kOutput, calls=%fused_computation.12 | convolution fusion | flops 12845248 | bytes 1573008 | tf_op jit(solution)/shard_map/hcm,hmde->hcde/dot_general | solution.py:63
  91.3 2.9 %multiply_convert_fusion = bf16[4,4,128,7,128]{2,4,3,1,0:T(8,128)(2,1)} fusion(f32[4,4,128,128]{2,3,1,0:T(8,128)S(1)} %convert_bitcast_fusion, f32[4,4,128,7]{2,3,1,0:T(8,128)S(1)} %fusion.36), kind=kLoop, calls=%fused_computation.1 | loop fusion | flops 3670016 | bytes 4775936 | tf_op jit(solution)/shard_map/convert_element_type | solution.py:116
  94.2 6.6 %fusion.4 = f32[5,4,128,128]{3,0,2,1:T(8,128)S(1)} fusion(bf16[32,4,128,128]{3,2,1,0:T(8,128)(2,1)} %bitcast.65, f32[32,4]{0,1:T(4,128)S(1)} %copy.45, pred[5,32]{1,0:T(8,128)(4,1)S(1)} %fusion.55), kind=kOutput, calls=%fused_computation.6 | convolution fusion | flops 125829760 | bytes 5505696 | tf_op jit(solution)/shard_map/jnh,nhde->jhde/dot_general | solution.py:98
  100.8 1.2 fusion.63
  102.0 1.1 fusion.21
  103.1 1.1 fusion.22
  104.1 1.1 fusion.23
  105.2 1.0 fusion.24
  106.2 1.1 fusion.25
  107.3 3.4 %fusion.2 = f32[4,4,128,128]{2,3,1,0:T(8,128)S(1)} fusion(bf16[4,4,128,896]{2,3,1,0:T(8,128)(2,1)S(1)} %bitcast.64, bf16[4,4,896,128]{3,1,2,0:T(4,128)(2,1)} %fusion.25), kind=kOutput, calls=%fused_computation.4 | convolution fusion | flops 469762048 | bytes 8388608 | tf_op jit(solution)/shard_map/hctk,hcke->hcte/dot_general | solution.py:118
  110.7 2.1 multiply_reduce_fusion
  112.8 1.3 fusion.10
  114.1 0.3 copy.49
  114.5 22.9 %all-gather.5.cloned.1.call-done = bf16[512,8192]{1,0:T(8,128)(2,1)} async-done(((bf16[512,256]{1,0:T(8,128)(2,1)}), bf16[512,8192]{1,0:T(8,128)(2,1)}) %all-gather.5.cloned.1.call-update) | async-done | bytes 8388624 | tf_op jit(solution)/shard_map/all_gather | solution.py:128
  137.4 10.1 %convolution_convert_fusion = bf16[512,8192]{1,0:T(8,128)(2,1)} fusion(bf16[512,8192]{1,0:T(8,128)(2,1)} %all-gather.5.cloned.1.call-done, bf16[64,8,4,128]{3,2,1,0:T(4,128)(2,1)S(1)} %bitcast.72), kind=kOutput, calls=%fused_computation | convolution fusion | flops 4299161600 | bytes 17301504 | tf_op jit(solution)/shard_map/dot_general | solution.py:126
  147.4 0.0 reduce-scatter.2.cloned.1.call-update
  147.4 94.5 %reduce-scatter.2.cloned.1.call-done = bf16[512,1024]{1,0:T(8,128)(2,1)} async-done(((bf16[512,8192]{1,0:T(8,128)(2,1)}), bf16[512,1024]{1,0:T(8,128)(2,1)}) %reduce-scatter.2.cloned.1.call-update) | async-done | bytes 1048592 | tf_op jit(solution)/shard_map/reduce_scatter | solution.py:131
  (29 shorter events, 0.1 us)
Async XLA Ops:
  6.5 77.8 %copy-start = (f32[4,8,16]{2,1,0:T(8,128)S(1)}, f32[4,8,16]{2,1,0:T(8,128)}, u32[]{:S(2)}) copy-start(f32[4,8,16]{2,1,0:T(8,128)} %param.14) | copy-start | bytes 6148
  6.5 87.7 %all-gather.7.cloned.1.call-start = ((), (), s32[]{:S(2)}) async-start(), calls=%async_computation.3 | async-start | bytes 4325376 | tf_op jit(solution)/shard_map/all_gather | solution.py:83
  9.1 7.1 %copy-start.6 = (u32[256]{0:T(256)S(1)}, u32[256]{0:T(256)}, u32[]{:S(2)}) copy-start(u32[256]{0:T(256)} %constant.43) | copy-start | bytes 3076
  9.2 74.6 %copy-start.2 = (bf16[512,512]{1,0:T(8,128)(2,1)S(1)}, bf16[512,512]{1,0:T(8,128)(2,1)}, u32[]{:S(2)}) copy-start(bf16[512,512]{1,0:T(8,128)(2,1)} %param.9) | copy-start | bytes 1572868
  10.8 73.5 %copy-start.4 = (s32[4,512]{1,0:T(4,128)S(1)}, s32[4,512]{1,0:T(4,128)}, u32[]{:S(2)}) copy-start(s32[4,512]{1,0:T(4,128)} %param.13) | copy-start | bytes 24580
  12.0 72.9 %copy-start.7 = (pred[4,4]{1,0:T(4,128)(4,1)S(1)}, pred[4,4]{1,0:T(4,128)(4,1)}, u32[]{:S(2)}) copy-start(pred[4,4]{1,0:T(4,128)(4,1)} %constant.36.clone) | copy-start | bytes 52
  14.7 73.4 %copy-start.5 = (pred[4,4]{1,0:T(4,128)(4,1)S(1)}, pred[4,4]{1,0:T(4,128)(4,1)}, u32[]{:S(2)}) copy-start(pred[4,4]{1,0:T(4,128)(4,1)} %constant.37.clone) | copy-start | bytes 52
  15.4 122.0 %all-gather.5.cloned.1.call-start = ((), (), s32[]{:S(2)}) async-start(), calls=%async_computation.1 | async-start | bytes 8650752 | tf_op jit(solution)/shard_map/all_gather | solution.py:128
  16.1 225.8 %reduce-scatter.2.cloned.1.call-start = ((), (), s32[]{:S(2)}) async-start(), calls=%async_computation.2 | async-start | bytes 9437184 | tf_op jit(solution)/shard_map/reduce_scatter | solution.py:131
  84.5 9.7 %copy-start.3 = (f32[4,8,4,128]{3,1,2,0:T(8,128)}, f32[4,8,4,128]{3,1,2,0:T(8,128)S(1)}, u32[]{:S(2)}) copy-start(f32[4,8,4,128]{3,1,2,0:T(8,128)S(1)} %convolution_bitcast_fusion) | copy-start | bytes 196612
  100.8 6.5 %copy-start.1 = (bf16[4,4,128,7,128]{2,4,3,1,0:T(8,128)(2,1)S(1)}, bf16[4,4,128,7,128]{2,4,3,1,0:T(8,128)(2,1)}, u32[]{:S(2)}) copy-start(bf16[4,4,128,7,128]{2,4,3,1,0:T(8,128)(2,1)} %multiply_convert_fusion) | copy-start | bytes 11010052
  107.3 3.4 %slice-start = ((f32[4,8,4,128]{3,1,2,0:T(8,128)}), f32[4,1,4,128]{3,1,2,0:T(1,128)S(1)}, s32[]{:S(2)}) async-start(f32[4,8,4,128]{3,1,2,0:T(8,128)} %copy-done.3), calls=%async_computation.4 | async-start | bytes 16384 | tf_op jit(solution)/shard_map/slice | solution.py:37
Sparse Core Ops, SparseCore 0:
  15.5 55.3 all-gather.6
  73.4 63.9 all-gather.4
  147.6 94.2 reduce-scatter.1
where the time goes:
time: 249 us; the launch traced here: 248 us
  waiting for transfers between devices  118 us (47%)
  blocking collectives  65.7 us (26%)
  matrix products  31.3 us (13%)
  between operations  14 us (6%)
  other arithmetic  12.2 us (5%)
  local copies, waits for them, and re-layouts  7.04 us (3%)
    reduce_scatter x1, waiting for transfers between devices, local(): lax.psum_scatter(projected.astype(jnp.bfloat16), 'head', scatter_dimensio...  94.5 us
    unnamed x1, blocking collectives  65.7 us
    all_gather x1, waiting for transfers between devices, local(): lax.all_gather(out_weight, 'ctx', axis=1, tiled=True)  22.9 us
    dot_general x1, matrix products, local(): jnp.dot(flattened, lax.all_gather(out_weight, 'ctx', axis=1, tiled=True),...  10.1 us
    dot_general x1, matrix products, local(): jnp.einsum('jnh,nhde->jhde', factors, block_rows, precision=lax.Precision...  6.6 us
    dot_general x2, matrix products, local(): jnp.einsum('hcm,hmde->hcde', factors, states, precision=lax.Precision.HIG...  6.35 us
  transfers between devices with their start and end apart: 3, of which 2 were waited for; matrix products, arithmetic and copies ran while one was open for 13% of the time, Pallas kernels for 0%

commit v1 on v0

v1 whole, which is shorter than its diff:
```python
import functools
import math

import jax
import jax.numpy as jnp
from jax import lax
from jax.experimental import pallas as pl
from jax.experimental.pallas import tpu as pltpu
from jax.sharding import PartitionSpec as P

HD = 128
BLOCK = 128
HL = 4
TOK = 512
NB = TOK // BLOCK
COLS = 256
MESH = pl.DeviceIdType.MESH
BF = jnp.bfloat16
F32 = jnp.float32


def kernel(
    X, Y, Z,
    q_ref, k_ref, v_ref, ld_ref, pick_ref, table_ref, w_ref, out_ref,
    qb, kb, vb, picks, wrows, bdrows, col, mix, lst, t0, t0p, d0, d0p, fall, xb, xd, yb, yd, rs, rb, ab, wb, acc, ob,
    in_sem, out_sem, w0s, w0r, w1s, w1r, w2s, w2r, wcs, wcr, cs, cr, xs, xr, ys, yr, rss, rsr, rings, ringr,
):
    R = X * Y
    RP = TOK // R
    xbits = X.bit_length() - 1
    ybits = Y.bit_length() - 1
    NR = 1 + xbits + ybits
    me = lax.axis_index("ctx")
    z = lax.axis_index("head")
    c = lax.rem(me, 2)
    chip = me // 2
    x = lax.rem(chip, X)
    y = chip // X
    plane = me // 4
    half = lax.rem(x, 2)
    mate = (me + 1 - 2 * c, z)
    right = lax.rem(z + 1, Z)
    left = lax.rem(z + Z - 1, Z)

    def at_x(step):
        return (y * X + lax.rem(x + step, X)) * 2 + c

    def at_y(step):
        return (lax.rem(y + step, Y) * X + x) * 2 + c

    def remote(src, dst, ssem, rsem, dev):
        return pltpu.make_async_remote_copy(
            src_ref=src, dst_ref=dst, send_sem=ssem, recv_sem=rsem, device_id=dev, device_id_type=MESH
        )

    loads = []
    for n, (src, dst) in enumerate(((k_ref, kb), (v_ref, vb), (q_ref, qb))):
        for h in range(HL):
            cp = pltpu.make_async_copy(src.at[:, h * HD:(h + 1) * HD], dst.at[h], in_sem.at[n, h])
            cp.start()
            loads.append(cp)

    barrier = pltpu.get_barrier_semaphore()

    def greet(ctx, head):
        pl.semaphore_signal(barrier, inc=1, device_id=(ctx, head), device_id_type=MESH)

    greet(mate[0], z)
    for s in range(1, X):
        greet(at_x(s), z)
    for s in range(1, Y):
        greet(at_y(s), z)
    greet(me, right)
    greet(me, left)

    def greet_sources(n, carry):
        ctx = 4 * z + 2 * (n // Z) + c
        head = lax.rem(n, Z)

        @pl.when(jnp.logical_or(ctx != me, head != z))
        def _():
            greet(ctx, head)

        return carry

    lax.fori_loop(0, 2 * Z, greet_sources, 0)

    for b in range(NB):
        wrows[b * HL:(b + 1) * HL, :] = ld_ref[:, b * BLOCK:(b + 1) * BLOCK]
        picks[b * HL:(b + 1) * HL, :] = pick_ref[:, b * BLOCK:(b + 1) * BLOCK]
    run = wrows[...]
    lane = lax.broadcasted_iota(jnp.int32, run.shape, 1)
    step = 1
    while step < BLOCK:
        run = run + jnp.where(lane >= step, pltpu.roll(run, step, 1), 0.0)
        step *= 2
    wrows[...] = run
    bdrows[...] = jnp.broadcast_to(run[:, BLOCK - 1:BLOCK], run.shape)
    d0[...] = jnp.zeros_like(d0)
    sub = lax.broadcasted_iota(jnp.int32, (8, BLOCK), 0)

    def prepare(h, carry):
        tab = table_ref[h]
        bd = [bdrows[pl.ds(b * HL + h, 1), :] for b in range(NB)]
        start = jnp.zeros_like(bd[0])
        rows = []
        for b in range(NB):
            pk = jnp.broadcast_to(picks[pl.ds(b * HL + h, 1), :], (8, BLOCK))
            lw = jnp.zeros((8, BLOCK), F32)
            for n in range(16):
                lw = jnp.where(pk == n, tab[:, n:n + 1], lw)
            wr = wrows[pl.ds(b * HL + h, 1), :]
            upper = jnp.where(sub >= 3, start, 0.0)
            if b == 3:
                upper = jnp.where(sub == 2, bd[2], upper)
            rows.append(lw * jnp.where(sub == 0, 1.0, jnp.exp(wr + upper)))
            rows.append(jnp.where(sub == 0, wr, jnp.where(sub == 1, jnp.exp(bd[b] - wr), 0.0)))
            start = start + bd[b]
        rows.append(jnp.zeros((BLOCK - 16 * NB, BLOCK), F32))
        col[h] = jnp.concatenate(rows, axis=0).T
        d0[pl.ds(h, 1), :] = start
        return carry

    lax.fori_loop(0, HL, prepare, 0)

    same = (plane == z).astype(jnp.int32)
    pl.semaphore_wait(barrier, 1 + (X - 1) + (Y - 1) + 2 + R - same)

    def w0_copy(r):
        return remote(
            w_ref.at[pl.ds(r * RP, RP), :],
            wb.at[r // X, lax.rem(r, X), c, half, z],
            w0s.at[r], w0r.at[half, z], (r * 2 + c, plane),
        )

    def w0_own():
        return pltpu.make_async_copy(
            w_ref.at[pl.ds(chip * RP, RP), :], wb.at[y, x, c, half, z], w0r.at[half, z]
        )

    def w0_send(n, carry):
        r = lax.rem(chip + 1 + n, R)
        own = jnp.logical_and(r == chip, plane == z)

        @pl.when(own)
        def _():
            w0_own().start()

        @pl.when(jnp.logical_not(own))
        def _():
            w0_copy(r).start()

        return carry

    lax.fori_loop(0, R, w0_send, 0)

    for cp in loads[:2 * HL]:
        cp.wait()

    def states(h, carry):
        s = []
        for b in range(NB):
            kk = kb[h, b * BLOCK:(b + 1) * BLOCK, :].astype(F32)
            kk = (kk * col[h, :, b * 16 + 9:b * 16 + 10]).astype(BF)
            s.append(lax.dot_general(
                kk, vb[h, b * BLOCK:(b + 1) * BLOCK, :], (((0,), (0,)), ((), ())), preferred_element_type=F32
            ))
        e = [jnp.exp(bdrows[pl.ds(b * HL + h, 1), :]) for b in range(NB)]
        pair = e[1] * s[0] + s[1]
        lst[h, 0] = s[0].astype(BF)
        lst[h, 1] = pair.astype(BF)
        lst[h, 2] = s[2].astype(BF)
        t0[h] = (e[3] * (e[2] * pair + s[2]) + s[3]).astype(BF)
        return carry

    lax.fori_loop(0, HL, states, 0)

    core_copies = [
        remote(t0, t0p, cs.at[0], cr.at[0], mate),
        remote(d0, d0p, cs.at[1], cr.at[1], mate),
    ]
    for cp in core_copies:
        cp.start()

    for cp in loads[2 * HL:]:
        cp.wait()
    causal = (
        lax.broadcasted_iota(jnp.int32, (BLOCK, BLOCK), 0) >= lax.broadcasted_iota(jnp.int32, (BLOCK, BLOCK), 1)
    )

    def inside(h):
        for b in range(NB):
            rows = slice(b * BLOCK, (b + 1) * BLOCK)
            qq = qb[h, rows, :]
            score = lax.dot_general(
                qq, kb[h, rows, :], (((1,), (1,)), ((), ())), preferred_element_type=F32
            )
            gap = col[h, :, b * 16 + 8:b * 16 + 9] - wrows[pl.ds(b * HL + h, 1), :]
            decay = jnp.where(causal, jnp.exp(jnp.where(causal, gap, 0.0)), 0.0)
            lhs = [(col[h, :, b * 16:b * 16 + 1] * decay * score).astype(BF)]
            rhs = [vb[h, rows, :]]
            qf = qq.astype(F32)
            if b & 1:
                lhs.append((qf * col[h, :, b * 16 + 1:b * 16 + 2]).astype(BF))
                rhs.append(lst[h, b - 1])
            if b & 2:
                lhs.append((qf * col[h, :, b * 16 + 2:b * 16 + 3]).astype(BF))
                rhs.append(lst[h, 1])
            mix[h, rows, :] = jnp.dot(
                jnp.concatenate(lhs, axis=1), jnp.concatenate(rhs, axis=0), preferred_element_type=F32
            )

    inside(0)

    for cp in core_copies:
        cp.wait_recv()
    first = jnp.exp(jnp.where(c == 0, d0[...], d0p[...]))
    second = jnp.exp(jnp.where(c == 0, d0p[...], d0[...]))
    d1 = d0[...] + d0p[...]
    xd[x] = d1
    fall[0] = first
    fall[1] = second
    for n in range(2):
        h = 2 * c + n
        sec = fall[1, pl.ds(h, 1), :]
        mine = t0[h].astype(F32) * jnp.where(c == 0, sec, 1.0)
        other = t0p[h].astype(F32) * jnp.where(c == 0, 1.0, sec)
        xb[x, n] = (mine + other).astype(BF)
    x_copies = []
    for s in range(1, X):
        dev = (at_x(s), z)
        src = lax.rem(x + X - s, X)
        for buf, i in ((xb, 0), (xd, 1)):
            cp = remote(buf.at[x], buf.at[x], xs.at[s - 1, i], xr.at[s - 1, i], dev)
            cp.start()
            got = remote(buf.at[src], buf.at[src], xs.at[s - 1, i], xr.at[s - 1, i], dev)
            x_copies.append((cp, got))
    for h in range(HL):
        rb[h, 0] = jnp.where(c == 1, t0p[h].astype(F32), 0.0).astype(BF)

    inside(1)

    for cp, got in x_copies:
        got.wait_recv()

    def weighted(buf, dec, n, at, size, before):
        h = 2 * c + n
        d = [dec[i, pl.ds(h, 1), :] for i in range(size)]
        ends, total = [], jnp.zeros_like(d[0])
        start = jnp.zeros_like(d[0])
        for i in range(size):
            start = start + jnp.where(i < at, d[i], 0.0)
            total = total + d[i]
            ends.append(total)
        f = [buf[i, n].astype(F32) for i in range(size)]
        near = [jnp.exp(jnp.minimum(start - ends[i], 0.0) + before) for i in range(size)]
        levels = []
        for bit in range(size.bit_length() - 1):
            top = (at >> bit) << bit
            low = top - (1 << bit)
            on = ((at >> bit) & 1) == 1
            part = jnp.zeros((HD, HD), F32)
            for i in range(size):
                take = jnp.logical_and(on, jnp.logical_and(i >= low, i < top))
                part = part + jnp.where(take, near[i], 0.0) * f[i]
            levels.append(part)
        whole = jnp.zeros((HD, HD), F32)
        for i in range(size):
            whole = whole + jnp.exp(total - ends[i]) * f[i]
        return levels, whole, start, total

    def keep(n, slot, value):
        h = 2 * c + n
        lower = fall[0, pl.ds(h, 1), :]
        rb[h, 1 + slot] = (value * jnp.where(c == 1, lower, 1.0)).astype(BF)
        rs[n, slot] = (value * jnp.where(c == 0, lower, 1.0)).astype(BF)

    offsets = []
    yd[y] = jnp.zeros((8, BLOCK), F32)
    for n in range(2):
        levels, whole, start, total = weighted(xb, xd, n, x, X, 0.0)
        for bit in range(xbits):
            keep(n, bit, levels[bit])
        yb[y, n] = whole.astype(BF)
        yd[y, pl.ds(2 * c + n, 1), :] = total
        offsets.append(start)
    y_copies = []
    for s in range(1, Y):
        dev = (at_y(s), z)
        src = lax.rem(y + Y - s, Y)
        for buf, i in ((yb, 0), (yd, 1)):
            cp = remote(buf.at[y], buf.at[y], ys.at[s - 1, i], yr.at[s - 1, i], dev)
            cp.start()
            got = remote(buf.at[src], buf.at[src], ys.at[s - 1, i], yr.at[s - 1, i], dev)
            y_copies.append((cp, got))

    inside(2)
    inside(3)

    for cp, got in y_copies:
        got.wait_recv()
    for n in range(2):
        levels, _, _, _ = weighted(yb, yd, n, y, Y, offsets[n])
        for bit in range(ybits):
            keep(n, xbits + bit, levels[bit])
    state_copy = remote(rs, rb.at[pl.ds(2 * c, 2), pl.ds(1, NR - 1)], rss.at[0], rsr.at[0], mate)
    state_got = remote(rs, rb.at[pl.ds(2 - 2 * c, 2), pl.ds(1, NR - 1)], rss.at[0], rsr.at[0], mate)
    state_copy.start()

    def w0_wait(n, carry):
        a, b = n // Z, lax.rem(n, Z)
        pltpu.make_async_copy(w_ref.at[pl.ds(0, RP), :], wb.at[y, x, c, a, b], w0r.at[a, b]).wait()
        return carry

    lax.fori_loop(0, 2 * Z, w0_wait, 0)
    w1 = []
    for s in range(1, X):
        piece, dev = wb.at[y, x, c, 0], (at_x(s), z)
        cp = remote(piece, piece, w1s.at[0, s - 1], w1r.at[0, s - 1], dev)
        cp.start()
        there = wb.at[y, lax.rem(x + X - s, X), c, 0]
        w1.append((cp, remote(there, there, w1s.at[0, s - 1], w1r.at[0, s - 1], dev)))
    for s in range(1, Y):
        piece, dev = wb.at[y, x, c, 1], (at_y(s), z)
        cp = remote(piece, piece, w1s.at[1, s - 1], w1r.at[1, s - 1], dev)
        cp.start()
        there = wb.at[lax.rem(y + Y - s, Y), x, c, 1]
        w1.append((cp, remote(there, there, w1s.at[1, s - 1], w1r.at[1, s - 1], dev)))

    H2 = Z // 2

    def travels(way, d, n):
        return d < H2 - 1 or (n < 2) == (way == 0)

    def ring(way, d, n):
        origin = lax.rem(z + (Z - d if way == 0 else d), Z)
        chunk = ab.at[origin, lax.rem(2 * c + n, HL)]
        dev = (me, right if way == 0 else left)
        return remote(chunk, chunk, rings.at[way, d, n], ringr.at[way, d, n], dev)

    def ring_got(way, d, n):
        origin = lax.rem(z + (Z - d - 1 if way == 0 else d + 1), Z)
        chunk = ab.at[origin, lax.rem(2 * c + n, HL)]
        dev = (me, right if way == 0 else left)
        return remote(chunk, chunk, rings.at[way, d, n], ringr.at[way, d, n], dev)

    def finish(h):
        for b in range(NB):
            rows = slice(b * BLOCK, (b + 1) * BLOCK)
            qf = qb[h, rows, :].astype(F32)
            lhs = jnp.concatenate(
                [(qf * col[h, :, b * 16 + 3 + n:b * 16 + 4 + n]).astype(BF) for n in range(NR)], axis=1
            )
            total = mix[h, rows, :] + jnp.dot(lhs, rb[h].reshape(NR * HD, HD), preferred_element_type=F32)
            mean = jnp.mean(total * total, axis=-1, keepdims=True)
            ab[z, h, rows, :] = (total * lax.rsqrt(mean + 1e-06)).astype(BF)

    for n in range(HL):
        if n == 2:
            state_got.wait_recv()
        finish(lax.rem(2 * c + n, HL))
        for way in range(2):
            if travels(way, 0, n):
                ring(way, 0, n).start()

    for cp, got in w1:
        got.wait_recv()
    w2 = []
    for s in range(1, Y):
        piece, dev = wb.at[y, :, c, 0], (at_y(s), z)
        cp = remote(piece, piece, w2s.at[0, s - 1], w2r.at[0, s - 1], dev)
        cp.start()
        there = wb.at[lax.rem(y + Y - s, Y), :, c, 0]
        w2.append((cp, remote(there, there, w2s.at[0, s - 1], w2r.at[0, s - 1], dev)))
    for s in range(1, X):
        piece, dev = wb.at[:, x, c, 1], (at_x(s), z)
        cp = remote(piece, piece, w2s.at[1, s - 1], w2r.at[1, s - 1], dev)
        cp.start()
        there = wb.at[:, lax.rem(x + X - s, X), c, 1]
        w2.append((cp, remote(there, there, w2s.at[1, s - 1], w2r.at[1, s - 1], dev)))
    wc = []

    def across(piece_of, way, s):
        cp = remote(piece_of(c), piece_of(c), wcs.at[way, s], wcr.at[way, s], mate)
        cp.start()
        other = piece_of(1 - c)
        wc.append((cp, remote(other, other, wcs.at[way, s], wcr.at[way, s], mate)))

    across(lambda core: wb.at[y, :, core, 0], 0, 0)
    across(lambda core: wb.at[:, x, core, 1], 1, 0)

    def w2_pass():
        for _, got in w2:
            got.wait_recv()
        for s in range(1, Y):
            across(lambda core: wb.at[lax.rem(y + Y - s, Y), :, core, 0], 0, s)
        for s in range(1, X):
            across(lambda core: wb.at[:, lax.rem(x + X - s, X), core, 1], 1, s)

    def project(origin, first, last=False):
        lhs = jnp.concatenate([ab[origin, h] for h in range(HL)], axis=1)

        def tile(u, carry):
            rhs = wb[:, :, lax.rem(u, 2), u // 2, origin].reshape(TOK, COLS)
            part = jnp.dot(lhs, rhs, preferred_element_type=F32)
            if not first:
                part = part + acc[u]
            if last:
                ob[u] = part.astype(BF)
                out_copy(u).start()
            else:
                acc[u] = part
            return carry

        lax.fori_loop(0, 4, tile, 0)

    def out_copy(u):
        return pltpu.make_async_copy(ob.at[u], out_ref.at[:, pl.ds(pl.multiple_of(u * COLS, COLS), COLS)], out_sem.at[u])

    waiting = [z]
    weights_here = False
    begun = False
    for d in range(H2):
        if d == H2 - 2 or (H2 == 1 and d == 0):
            w2_pass()
        for n in range(HL):
            for way in range(2):
                if travels(way, d, n):
                    ring_got(way, d, n).wait_recv()
                    if d + 1 < H2 and travels(way, d + 1, n):
                        ring(way, d + 1, n).start()
            if weights_here:
                for _ in range(2):
                    if waiting:
                        project(waiting.pop(0), not begun)
                        begun = True
            elif d >= H2 - 2:
                for cp, got in wc:
                    got.wait_recv()
                weights_here = True
        if d + 1 < H2:
            waiting.append(lax.rem(z + Z - d - 1, Z))
            waiting.append(lax.rem(z + d + 1, Z))
    while waiting:
        project(waiting.pop(0), not begun)
        begun = True
    project(lax.rem(z + H2, Z), False, True)

    def w0_sent(n, carry):
        own = jnp.logical_and(n == chip, plane == z)

        @pl.when(jnp.logical_not(own))
        def _():
            w0_copy(n).wait_send()

        return carry

    lax.fori_loop(0, R, w0_sent, 0)
    for cp in core_copies:
        cp.wait_send()
    state_copy.wait_send()
    for cp, _ in x_copies + y_copies + w1 + w2 + wc:
        cp.wait_send()
    for way in range(2):
        for d in range(H2):
            for n in range(HL):
                if travels(way, d, n):
                    ring(way, d, n).wait_send()
    for u in range(4):
        out_copy(u).wait()


def local(X, Y, Z, queries, keys, values, log_decay, level_pick, level_table, out_weight):
    R = X * Y
    NR = 1 + (X.bit_length() - 1) + (Y.bit_length() - 1)
    H2 = Z // 2
    anyspace = pl.BlockSpec(memory_space=pl.ANY)
    vmem = pl.BlockSpec(memory_space=pltpu.VMEM)
    dma = pltpu.SemaphoreType.DMA
    heads = (HL, TOK, HD)
    state = (HD, HD)
    scratch = [
        pltpu.VMEM(heads, BF), pltpu.VMEM(heads, BF), pltpu.VMEM(heads, BF),
        pltpu.VMEM((NB * HL, BLOCK), jnp.int32), pltpu.VMEM((NB * HL, BLOCK), F32), pltpu.VMEM((NB * HL, BLOCK), F32),
        pltpu.VMEM((HL, BLOCK, BLOCK), F32),
        pltpu.VMEM(heads, F32),
        pltpu.VMEM((HL, 3) + state, BF),
        pltpu.VMEM((HL,) + state, BF), pltpu.VMEM((HL,) + state, BF),
        pltpu.VMEM((8, BLOCK), F32), pltpu.VMEM((8, BLOCK), F32), pltpu.VMEM((2, 8, BLOCK), F32),
        pltpu.VMEM((X, 2) + state, BF), pltpu.VMEM((X, 8, BLOCK), F32),
        pltpu.VMEM((Y, 2) + state, BF), pltpu.VMEM((Y, 8, BLOCK), F32),
        pltpu.VMEM((2, NR - 1) + state, BF), pltpu.VMEM((HL, NR) + state, BF),
        pltpu.VMEM((Z,) + heads, BF),
        pltpu.VMEM((Y, X, 2, 2, Z, TOK // R, COLS), BF),
        pltpu.VMEM((4, TOK, COLS), F32), pltpu.VMEM((4, TOK, COLS), BF),
        dma((3, HL)), dma((4,)),
        dma((R,)), dma((2, Z)),
        dma((2, max(X, Y))), dma((2, max(X, Y))),
        dma((2, max(X, Y))), dma((2, max(X, Y))),
        dma((2, max(X, Y))), dma((2, max(X, Y))),
        dma((2,)), dma((2,)),
        dma((X, 2)), dma((X, 2)),
        dma((Y, 2)), dma((Y, 2)),
        dma((1,)), dma((1,)),
        dma((2, H2, HL)), dma((2, H2, HL)),
    ]
    return pl.pallas_call(
        functools.partial(kernel, X, Y, Z),
        out_shape=jax.ShapeDtypeStruct((TOK, 4 * COLS), BF),
        in_specs=[anyspace, anyspace, anyspace, vmem, vmem, vmem, anyspace],
        out_specs=anyspace,
        scratch_shapes=scratch,
        cost_estimate=pl.CostEstimate(flops=5_000_000_000, bytes_accessed=4_000_000, transcendentals=1_000_000),
        compiler_params=pltpu.CompilerParams(
            collective_id=0, has_side_effects=True, vmem_limit_bytes=48 * 1024 * 1024
        ),
    )(queries, keys, values, log_decay, level_pick, level_table, out_weight)


def solution(mesh):
    nctx, Z = mesh.shape["ctx"], mesh.shape["head"]
    chips = nctx // 2
    X = 1 << int(math.log2(chips)) // 2
    Y = chips // X
    in_specs = (
        P("ctx", "head"),
        P("ctx", "head"),
        P("ctx", "head"),
        P("head", "ctx"),
        P("head", "ctx"),
        P("head", None, None),
        P("head", "ctx"),
    )
    return jax.shard_map(
        functools.partial(local, X, Y, Z), mesh=mesh, in_specs=in_specs, out_specs=P("ctx", "head"), check_vma=False
    )
```

time: 249 us -> 97.6 us (0.39)
  the two profiles are of different devices: /device:TPU:1 before, /device:TPU:103 now
where the time goes in v1:
time: 97.6 us; the launch traced here: 97.2 us
  Pallas kernels  90.1 us (92%)
  local copies, waits for them, and re-layouts  7.15 us (7%)
    pallas_call x1, Pallas kernels, local(): pl.pallas_call(functools.partial(kernel, X, Y, Z), out_shape=jax.ShapeDty...  90.1 us
    unnamed x15, local copies, waits for them, and re-layouts  7.15 us

profile of v1, /device:TPU:103, one launch (start us, length us, event | category | flops | bytes accessed | tf_op | source)
XLA Modules:
  0.0 97.2 jit_solution(3748875299025667885)
XLA Ops:
  0.0 0.0 copy-start
  0.0 1.0 %copy-done = bf16[512,512]{1,0:T(8,128)(2,1)S(1)} copy-done((bf16[512,512]{1,0:T(8,128)(2,1)S(1)}, bf16[512,512]{1,0:T(8,128)(2,1)}, u32[]{:S(2)}) %copy-start) | copy-done | bytes 524312
  1.0 0.0 copy-start.1
  1.0 1.0 %copy-done.1 = bf16[512,512]{1,0:T(8,128)(2,1)S(1)} copy-done((bf16[512,512]{1,0:T(8,128)(2,1)S(1)}, bf16[512,512]{1,0:T(8,128)(2,1)}, u32[]{:S(2)}) %copy-start.1) | copy-done | bytes 524312
  2.1 0.0 copy-start.2
  2.1 1.0 %copy-done.2 = bf16[512,512]{1,0:T(8,128)(2,1)S(1)} copy-done((bf16[512,512]{1,0:T(8,128)(2,1)S(1)}, bf16[512,512]{1,0:T(8,128)(2,1)}, u32[]{:S(2)}) %copy-start.2) | copy-done | bytes 524312
  3.1 0.0 copy-start.3
  3.1 0.9 copy-done.3
  4.1 0.0 copy-start.4
  4.1 0.7 copy-done.4
  4.8 0.0 copy-start.5
  4.8 0.7 copy-done.5
  5.5 0.0 copy-start.6
  5.5 0.7 copy-done.6
  6.2 90.1 %shard_map.73 = bf16[512,1024]{1,0:T(8,128)(2,1)S(1)} custom-call(bf16[512,512]{1,0:T(8,128)(2,1)S(1)} %copy-done, bf16[512,512]{1,0:T(8,128)(2,1)S(1)} %copy-done.1, bf16[512,512]{1,0:T(8,128)(2,1)S(1)} %copy-done.2, f32[4,512]{1,0:T(4,128)S(1)} %copy-done.5, s32[4,512]{1,0:T(4,128)S(1)} %copy-done.6, f32[4,8,16]{2,1,0:T(8,128)S(1)} %copy-done.4, ...), custom_call_target="tpu_custom_call" | custom-call | flops 5000000000 | bytes 4000000 | tf_op jit(solution)/shard_map/pallas_call | solution.py:507
  96.3 1.0 %copy.9 = bf16[512,1024]{1,0:T(8,128)(2,1)} copy(bf16[512,1024]{1,0:T(8,128)(2,1)S(1)} %shard_map.73) | data formatting | bytes 2097152
Async XLA Ops:
  0.0 1.0 %copy-start = (bf16[512,512]{1,0:T(8,128)(2,1)S(1)}, bf16[512,512]{1,0:T(8,128)(2,1)}, u32[]{:S(2)}) copy-start(bf16[512,512]{1,0:T(8,128)(2,1)} %q_ref.1) | copy-start | bytes 1572868
  1.0 1.0 %copy-start.1 = (bf16[512,512]{1,0:T(8,128)(2,1)S(1)}, bf16[512,512]{1,0:T(8,128)(2,1)}, u32[]{:S(2)}) copy-start(bf16[512,512]{1,0:T(8,128)(2,1)} %k_ref.1) | copy-start | bytes 1572868
  2.1 1.0 %copy-start.2 = (bf16[512,512]{1,0:T(8,128)(2,1)S(1)}, bf16[512,512]{1,0:T(8,128)(2,1)}, u32[]{:S(2)}) copy-start(bf16[512,512]{1,0:T(8,128)(2,1)} %v_ref.1) | copy-start | bytes 1572868
  3.1 0.9 copy-start.3
  4.1 0.7 copy-start.4
  4.8 0.7 copy-start.5
  5.5 0.7 copy-start.6

commit v2 on v1

v2 whole, which is shorter than its diff:
```python
import functools
import math

import jax
import jax.numpy as jnp
from jax import lax
from jax.experimental import pallas as pl
from jax.experimental.pallas import tpu as pltpu
from jax.sharding import PartitionSpec as P

HD = 128
BLOCK = 128
HL = 4
TOK = 512
NB = TOK // BLOCK
COLS = 256
W2_SLOT, W3_SLOTS = 2, (5, 7, 9)
MESH = pl.DeviceIdType.MESH
BF = jnp.bfloat16
F32 = jnp.float32


def kernel(
    X, Y, Z,
    q_ref, k_ref, v_ref, ld_hbm, pick_hbm, table_hbm, w_ref, out_ref,
    ld_ref, pick_ref, table_ref,
    qb, kb, vb, picks, wrows, bdrows, col, mix, lst, stage, t0, t0p, d0, d0p, fall, xb, xd, yb, yd, rs, rb, ab, wb, acc, ob,
    in_sem, out_sem, wqs, wqr, w0s, w0r, w1s, w1r, w2s, w2r, wcs, wcr, cs, cr, xs, xr, ys, yr, rss, rsr, rings, ringr,
):
    R = X * Y
    RP = TOK // R
    xbits = X.bit_length() - 1
    ybits = Y.bit_length() - 1
    NR = 1 + xbits + ybits
    me = lax.axis_index("ctx")
    z = lax.axis_index("head")
    c = lax.rem(me, 2)
    chip = me // 2
    x = lax.rem(chip, X)
    y = chip // X
    half = lax.rem(x, 2)
    mate = (me + 1 - 2 * c, z)
    right = lax.rem(z + 1, Z)
    left = lax.rem(z + Z - 1, Z)

    def at_x(step):
        return (y * X + lax.rem(x + step, X)) * 2 + c

    def at_y(step):
        return (lax.rem(y + step, Y) * X + x) * 2 + c

    def remote(src, dst, ssem, rsem, dev):
        return pltpu.make_async_remote_copy(
            src_ref=src, dst_ref=dst, send_sem=ssem, recv_sem=rsem, device_id=dev, device_id_type=MESH
        )

    barrier = pltpu.get_barrier_semaphore()

    def greet(ctx, head):
        pl.semaphore_signal(barrier, inc=1, device_id=(ctx, head), device_id_type=MESH)

    greet(mate[0], z)
    for s in range(1, X):
        greet(at_x(s), z)
    for s in range(1, Y):
        greet(at_y(s), z)
    greet(me, right)
    greet(me, left)

    for n in range(2):
        for head in range(Z):
            greet((y * X + 2 * lax.rem(z, 2) + n) * 2 + c, head)

    small = [
        pltpu.make_async_copy(src, dst, in_sem.at[3, n])
        for n, (src, dst) in enumerate(((ld_hbm, ld_ref), (pick_hbm, pick_ref), (table_hbm, table_ref)))
    ]
    for cp in small:
        cp.start()
    loads = []
    for n, (src, dst) in enumerate(((k_ref, kb), (v_ref, vb), (q_ref, qb))):
        for h in range(HL):
            cp = pltpu.make_async_copy(src.at[:, h * HD:(h + 1) * HD], dst.at[h], in_sem.at[n, h])
            cp.start()
            loads.append(cp)

    for cp in small:
        cp.wait()

    for b in range(NB):
        wrows[b * HL:(b + 1) * HL, :] = ld_ref[:, b * BLOCK:(b + 1) * BLOCK]
        picks[b * HL:(b + 1) * HL, :] = pick_ref[:, b * BLOCK:(b + 1) * BLOCK]
    run = wrows[...]
    lane = lax.broadcasted_iota(jnp.int32, run.shape, 1)
    step = 1
    while step < BLOCK:
        run = run + jnp.where(lane >= step, pltpu.roll(run, step, 1), 0.0)
        step *= 2
    wrows[...] = run
    bdrows[...] = jnp.broadcast_to(run[:, BLOCK - 1:BLOCK], run.shape)
    d0[...] = jnp.zeros_like(d0)
    sub = lax.broadcasted_iota(jnp.int32, (8, BLOCK), 0)

    def prepare(h, carry):
        tab = table_ref[h]
        bd = [bdrows[pl.ds(b * HL + h, 1), :] for b in range(NB)]
        start = jnp.zeros_like(bd[0])
        rows = []
        for b in range(NB):
            pk = jnp.broadcast_to(picks[pl.ds(b * HL + h, 1), :], (8, BLOCK))
            lw = jnp.zeros((8, BLOCK), F32)
            for n in range(16):
                lw = jnp.where(pk == n, tab[:, n:n + 1], lw)
            wr = wrows[pl.ds(b * HL + h, 1), :]
            upper = jnp.where(sub >= 3, start, 0.0)
            if b == 3:
                upper = jnp.where(sub == 2, bd[2], upper)
            rows.append(lw * jnp.where(sub == 0, 1.0, jnp.exp(wr + upper)))
            rows.append(jnp.where(sub == 0, wr, jnp.where(sub == 1, jnp.exp(bd[b] - wr), 0.0)))
            start = start + bd[b]
        rows.append(jnp.zeros((BLOCK - 16 * NB, BLOCK), F32))
        col[h] = jnp.concatenate(rows, axis=0).T
        d0[pl.ds(h, 1), :] = start
        return carry

    lax.fori_loop(0, HL, prepare, 0)

    for cp in loads[:2 * HL]:
        cp.wait()

    def states(h, carry):
        s = []
        for b in range(NB):
            kk = kb[h, b * BLOCK:(b + 1) * BLOCK, :].astype(F32)
            kk = (kk * col[h, :, b * 16 + 9:b * 16 + 10]).astype(BF)
            s.append(lax.dot_general(
                kk, vb[h, b * BLOCK:(b + 1) * BLOCK, :], (((0,), (0,)), ((), ())), preferred_element_type=F32
            ))
        e = [jnp.exp(bdrows[pl.ds(b * HL + h, 1), :]) for b in range(NB)]
        pair = e[1] * s[0] + s[1]
        lst[h, 0] = s[0].astype(BF)
        lst[h, 1] = pair.astype(BF)
        lst[h, 2] = s[2].astype(BF)
        t0[h] = (e[3] * (e[2] * pair + s[2]) + s[3]).astype(BF)
        return carry

    lax.fori_loop(0, HL, states, 0)

    pl.semaphore_wait(barrier, 1 + (X - 1) + (Y - 1) + 2 + R)

    QR = TOK // Y

    def w_quarter(row):
        return w_ref.at[pl.ds(pl.multiple_of(row * QR, QR), QR), :]

    wq = [pltpu.make_async_copy(w_quarter(y), stage.at[y], wqr.at[0])]
    wq_got = [wq[0]]
    for s in range(1, Y):
        dev = (at_y(s), z)
        src = lax.rem(y + Y - s, Y)
        wq.append(remote(w_quarter(lax.rem(y + s, Y)), stage.at[y], wqs.at[s], wqr.at[s], dev))
        wq_got.append(remote(w_quarter(y), stage.at[src], wqs.at[s], wqr.at[s], dev))
    for cp in wq:
        cp.start()

    def w0_place(n):
        row, col_at = lax.rem(n // X + y, Y), lax.rem(n + x, X)
        plane = 2 * row + x // 2
        return row, col_at, plane, jnp.logical_and(plane == z, col_at == x)

    def w0_copy(n):
        row, col_at, plane, _ = w0_place(n)
        return remote(
            stage.at[row, pl.ds(pl.multiple_of(col_at * RP, RP), RP), :],
            wb.at[y, col_at, c, half, z],
            w0s.at[n], w0r.at[half, z], ((y * X + col_at) * 2 + c, plane),
        )

    def w0_send(n, carry):
        row, col_at, plane, own = w0_place(n)

        @pl.when(own)
        def _():
            pltpu.make_async_copy(
                stage.at[row, pl.ds(pl.multiple_of(col_at * RP, RP), RP), :],
                wb.at[y, col_at, c, half, z], w0r.at[half, z],
            ).start()

        @pl.when(jnp.logical_not(own))
        def _():
            w0_copy(n).start()

        return carry

    def w0_pass():
        wq_got[0].wait()
        for got in wq_got[1:]:
            got.wait_recv()
        lax.fori_loop(0, R, w0_send, 0)

    core_copies = [
        remote(t0, t0p, cs.at[0], cr.at[0], mate),
        remote(d0, d0p, cs.at[1], cr.at[1], mate),
    ]
    for cp in core_copies:
        cp.start()

    for cp in loads[2 * HL:]:
        cp.wait()
    causal = (
        lax.broadcasted_iota(jnp.int32, (BLOCK, BLOCK), 0) >= lax.broadcasted_iota(jnp.int32, (BLOCK, BLOCK), 1)
    )

    def inside(h):
        for b in range(NB):
            rows = slice(b * BLOCK, (b + 1) * BLOCK)
            qq = qb[h, rows, :]
            score = lax.dot_general(
                qq, kb[h, rows, :], (((1,), (1,)), ((), ())), preferred_element_type=F32
            )
            gap = col[h, :, b * 16 + 8:b * 16 + 9] - wrows[pl.ds(b * HL + h, 1), :]
            decay = jnp.where(causal, jnp.exp(jnp.where(causal, gap, 0.0)), 0.0)
            lhs = [(col[h, :, b * 16:b * 16 + 1] * decay * score).astype(BF)]
            rhs = [vb[h, rows, :]]
            qf = qq.astype(F32)
            if b & 1:
                lhs.append((qf * col[h, :, b * 16 + 1:b * 16 + 2]).astype(BF))
                rhs.append(lst[h, b - 1])
            if b & 2:
                lhs.append((qf * col[h, :, b * 16 + 2:b * 16 + 3]).astype(BF))
                rhs.append(lst[h, 1])
            mix[h, rows, :] = jnp.dot(
                jnp.concatenate(lhs, axis=1), jnp.concatenate(rhs, axis=0), preferred_element_type=F32
            )

    for cp in core_copies:
        cp.wait_recv()
    fall[0] = jnp.exp(jnp.where(c == 0, d0[...], d0p[...]))
    fall[1] = jnp.exp(jnp.where(c == 0, d0p[...], d0[...]))
    xd[x] = d0[...] + d0p[...]

    def spread(bufs, at, size, ssem, rsem, dev_of, n):
        copies = []
        state, decays = bufs
        for s in range(1, size):
            src = lax.rem(at + size - s, size)
            pieces = [(state.at[at, n], state.at[src, n], n)]
            if n == 0:
                pieces.append((decays.at[at], decays.at[src], 2))
            for mine, theirs, i in pieces:
                cp = remote(mine, mine, ssem.at[s - 1, i], rsem.at[s - 1, i], (dev_of(s), z))
                cp.start()
                copies.append((cp, remote(theirs, theirs, ssem.at[s - 1, i], rsem.at[s - 1, i], (dev_of(s), z))))
        return copies

    x_copies = []
    for n in range(2):
        h = 2 * c + n
        sec = fall[1, pl.ds(h, 1), :]
        mine = t0[h].astype(F32) * jnp.where(c == 0, sec, 1.0)
        other = t0p[h].astype(F32) * jnp.where(c == 0, 1.0, sec)
        xb[x, n] = (mine + other).astype(BF)
        x_copies.append(spread((xb, xd), x, X, xs, xr, at_x, n))
    for h in range(HL):
        rb[h, 0] = jnp.where(c == 1, t0p[h].astype(F32), 0.0).astype(BF)

    inside(0)
    inside(1)
    w0_pass()

    def weighted(buf, dec, n, at, size, before, last):
        h = 2 * c + n
        d = [dec[i, pl.ds(h, 1), :] for i in range(size)]
        ends, total = [], jnp.zeros_like(d[0])
        start = jnp.zeros_like(d[0])
        for i in range(size):
            start = start + jnp.where(i < at, d[i], 0.0)
            total = total + d[i]
            ends.append(total)
        f = [buf[i, n].astype(F32) for i in range(size)]
        near = [jnp.exp(jnp.minimum(start - ends[i], 0.0) + before) for i in range(size)]
        levels = []
        for bit in range(size.bit_length() - 1):
            top = (at >> bit) << bit
            low = top - (1 << bit)
            on = ((at >> bit) & 1) == 1
            part = jnp.zeros((HD, HD), F32)
            for i in range(size):
                take = jnp.logical_and(on, jnp.logical_and(i >= low, i < top))
                part = part + jnp.where(take, near[i], 0.0) * f[i]
            levels.append(part)
        if last:
            return levels
        whole = jnp.zeros((HD, HD), F32)
        for i in range(size):
            whole = whole + jnp.exp(total - ends[i]) * f[i]
        return levels, whole, start

    def keep(n, slot, value):
        h = 2 * c + n
        lower = fall[0, pl.ds(h, 1), :]
        rb[h, 1 + slot] = (value * jnp.where(c == 1, lower, 1.0)).astype(BF)
        rs[n, slot] = (value * jnp.where(c == 0, lower, 1.0)).astype(BF)

    offsets, y_copies = [], []
    for n in range(2):
        for cp, got in x_copies[n]:
            got.wait_recv()
        if n == 0:
            yd[y] = sum(xd[i] for i in range(X))
        levels, whole, start = weighted(xb, xd, n, x, X, 0.0, False)
        yb[y, n] = whole.astype(BF)
        y_copies.append(spread((yb, yd), y, Y, ys, yr, at_y, n))
        offsets.append(start)
        for bit in range(xbits):
            keep(n, bit, levels[bit])

    inside(2)
    inside(3)

    def w0_wait(n, carry):
        a, b = n // Z, lax.rem(n, Z)
        pltpu.make_async_copy(w_ref.at[pl.ds(0, RP), :], wb.at[y, x, c, a, b], w0r.at[a, b]).wait()
        return carry

    w1 = []

    def w1_pass():
        lax.fori_loop(0, 2 * Z, w0_wait, 0)
        for s in range(1, X):
            piece, dev = wb.at[y, x, c, 0], (at_x(s), z)
            cp = remote(piece, piece, w1s.at[0, s - 1], w1r.at[0, s - 1], dev)
            cp.start()
            there = wb.at[y, lax.rem(x + X - s, X), c, 0]
            w1.append((cp, remote(there, there, w1s.at[0, s - 1], w1r.at[0, s - 1], dev)))
        for s in range(1, Y):
            piece, dev = wb.at[y, x, c, 1], (at_y(s), z)
            cp = remote(piece, piece, w1s.at[1, s - 1], w1r.at[1, s - 1], dev)
            cp.start()
            there = wb.at[lax.rem(y + Y - s, Y), x, c, 1]
            w1.append((cp, remote(there, there, w1s.at[1, s - 1], w1r.at[1, s - 1], dev)))

    H2 = Z // 2

    def travels(way, d, n):
        return d < H2 - 1 or (n < 2) == (way == 0)

    def ring(way, d, n):
        origin = lax.rem(z + (Z - d if way == 0 else d), Z)
        chunk = ab.at[origin, lax.rem(2 * c + n, HL)]
        dev = (me, right if way == 0 else left)
        return remote(chunk, chunk, rings.at[way, d, n], ringr.at[way, d, n], dev)

    def ring_got(way, d, n):
        origin = lax.rem(z + (Z - d - 1 if way == 0 else d + 1), Z)
        chunk = ab.at[origin, lax.rem(2 * c + n, HL)]
        dev = (me, right if way == 0 else left)
        return remote(chunk, chunk, rings.at[way, d, n], ringr.at[way, d, n], dev)

    def finish(h):
        for b in range(NB):
            rows = slice(b * BLOCK, (b + 1) * BLOCK)
            qf = qb[h, rows, :].astype(F32)
            lhs = jnp.concatenate(
                [(qf * col[h, :, b * 16 + 3 + n:b * 16 + 4 + n]).astype(BF) for n in range(NR)], axis=1
            )
            total = mix[h, rows, :] + jnp.dot(lhs, rb[h].reshape(NR * HD, HD), preferred_element_type=F32)
            mean = jnp.mean(total * total, axis=-1, keepdims=True)
            ab[z, h, rows, :] = (total * lax.rsqrt(mean + 1e-06)).astype(BF)

    def state_copy(n, h):
        return remote(rs.at[n], rb.at[h + n, pl.ds(1, NR - 1)], rss.at[n], rsr.at[n], mate)

    for n in range(HL):
        if n < 2:
            for cp, got in y_copies[n]:
                got.wait_recv()
            levels = weighted(yb, yd, n, y, Y, offsets[n], True)
            for bit in range(ybits):
                keep(n, xbits + bit, levels[bit])
            state_copy(n, 2 * c).start()
        else:
            state_copy(n - 2, 2 - 2 * c).wait_recv()
        finish(lax.rem(2 * c + n, HL))
        for way in range(2):
            if travels(way, 0, n):
                ring(way, 0, n).start()
    w1_pass()

    w2 = {}
    wc = []

    def block(axis, at, part, core):
        if axis == 0:
            return wb.at[at, :, core, 0] if part is None else wb.at[at, pl.ds(part * (X // 2), X // 2), core, 0]
        return wb.at[:, at, core, 1] if part is None else wb.at[pl.ds(part * (Y // 2), Y // 2), at, core, 1]

    def across(axis, at, part):
        n = len(wc)
        cp = remote(block(axis, at, part, c), block(axis, at, part, c), wcs.at[n], wcr.at[n], mate)
        cp.start()
        other = block(axis, at, part, 1 - c)
        wc.append((cp, remote(other, other, wcs.at[n], wcr.at[n], mate)))

    def near(axis, s):
        size, at = (Y, y) if axis == 0 else (X, x)
        return lax.rem(at + s + size, size)

    def w2_copy(axis, way, k):
        sign = 1 - 2 * way
        part = way if k != 1 else 1 - way
        dev = (at_y(sign % Y) if axis == 0 else at_x(sign % X), z)
        sems = (w2s.at[axis, way, k], w2r.at[axis, way, k])
        mine = block(axis, near(axis, 0 if k < 2 else -sign), part, c)
        at = near(axis, -sign if k < 2 else -2 * sign)
        theirs = block(axis, at, part, c)
        cp = remote(mine, mine, *sems, dev)
        cp.start()
        w2[axis, way, k] = (cp, remote(theirs, theirs, *sems, dev), at, part)

    def w2_pass():
        for cp, got in w1:
            got.wait_recv()
        for k in range(2):
            for axis in range(2):
                for way in range(2):
                    w2_copy(axis, way, k)
        across(0, y, None)
        across(1, x, None)

    def w3_pass(k):
        for axis in range(2):
            for way in range(2):
                _, got, at, part = w2[axis, way, k]
                got.wait_recv()
                if k == 0:
                    w2_copy(axis, way, 2)
                across(axis, at, part)

    def project(origins, first, last=False):
        def tile(u, carry):
            lhs = jnp.concatenate([ab[origin, h] for origin in origins for h in range(HL)], axis=1)
            rhs = jnp.concatenate(
                [wb[:, :, lax.rem(u, 2), u // 2, origin].reshape(TOK, COLS) for origin in origins], axis=0
            )
            part = jnp.dot(lhs, rhs, preferred_element_type=F32)
            if not first:
                part = part + acc[u]
            if last:
                ob[u] = part.astype(BF)
                out_copy(u).start()
            else:
                acc[u] = part
            return carry

        lax.fori_loop(0, 4, tile, 0)

    def out_copy(u):
        return pltpu.make_async_copy(ob.at[u], out_ref.at[:, pl.ds(pl.multiple_of(u * COLS, COLS), COLS)], out_sem.at[u])

    waiting = [[z]]
    begun = False
    for d in range(H2):
        for n in range(HL):
            for way in range(2):
                if travels(way, d, n):
                    ring_got(way, d, n).wait_recv()
                    if d + 1 < H2 and travels(way, d + 1, n):
                        ring(way, d + 1, n).start()
            slot = d * HL + n
            if slot == W2_SLOT:
                w2_pass()
            for k in range(3):
                if slot == W3_SLOTS[k]:
                    w3_pass(k)
            if slot == W3_SLOTS[2] + 1:
                for _, got in wc:
                    got.wait_recv()
            if slot > W3_SLOTS[2] and waiting:
                project(waiting.pop(0), not begun)
                begun = True
        if d + 1 < H2:
            waiting.append([lax.rem(z + Z - d - 1, Z), lax.rem(z + d + 1, Z)])
    while waiting:
        project(waiting.pop(0), not begun)
        begun = True
    project([lax.rem(z + H2, Z)], False, True)

    def w0_sent(n, carry):
        @pl.when(jnp.logical_not(w0_place(n)[3]))
        def _():
            w0_copy(n).wait_send()

        return carry

    lax.fori_loop(0, R, w0_sent, 0)
    for cp in core_copies + wq[1:]:
        cp.wait_send()
    for n in range(2):
        state_copy(n, 2 * c).wait_send()
    for cp, _ in x_copies[0] + x_copies[1] + y_copies[0] + y_copies[1] + w1 + wc + [(cp, 0) for cp, _, _, _ in w2.values()]:
        cp.wait_send()
    for way in range(2):
        for d in range(H2):
            for n in range(HL):
                if travels(way, d, n):
                    ring(way, d, n).wait_send()
    for u in range(4):
        out_copy(u).wait()


def local(X, Y, Z, queries, keys, values, log_decay, level_pick, level_table, out_weight):
    R = X * Y
    NR = 1 + (X.bit_length() - 1) + (Y.bit_length() - 1)
    H2 = Z // 2
    anyspace = pl.BlockSpec(memory_space=pl.ANY)
    dma = pltpu.SemaphoreType.DMA
    heads = (HL, TOK, HD)
    state = (HD, HD)
    scratch = [
        pltpu.VMEM((HL, TOK), F32), pltpu.VMEM((HL, TOK), jnp.int32), pltpu.VMEM(level_table.shape, F32),
        pltpu.VMEM(heads, BF), pltpu.VMEM(heads, BF), pltpu.VMEM(heads, BF),
        pltpu.VMEM((NB * HL, BLOCK), jnp.int32), pltpu.VMEM((NB * HL, BLOCK), F32), pltpu.VMEM((NB * HL, BLOCK), F32),
        pltpu.VMEM((HL, BLOCK, BLOCK), F32),
        pltpu.VMEM(heads, F32),
        pltpu.VMEM((HL, 3) + state, BF),
        pltpu.VMEM((Y, TOK // Y, COLS), BF),
        pltpu.VMEM((HL,) + state, BF), pltpu.VMEM((HL,) + state, BF),
        pltpu.VMEM((8, BLOCK), F32), pltpu.VMEM((8, BLOCK), F32), pltpu.VMEM((2, 8, BLOCK), F32),
        pltpu.VMEM((X, 2) + state, BF), pltpu.VMEM((X, 8, BLOCK), F32),
        pltpu.VMEM((Y, 2) + state, BF), pltpu.VMEM((Y, 8, BLOCK), F32),
        pltpu.VMEM((2, NR - 1) + state, BF), pltpu.VMEM((HL, NR) + state, BF),
        pltpu.VMEM((Z,) + heads, BF),
        pltpu.VMEM((Y, X, 2, 2, Z, TOK // R, COLS), BF),
        pltpu.VMEM((4, TOK, COLS), F32), pltpu.VMEM((4, TOK, COLS), BF),
        dma((4, HL)), dma((4,)),
        dma((Y,)), dma((Y,)),
        dma((R,)), dma((2, Z)),
        dma((2, max(X, Y))), dma((2, max(X, Y))),
        dma((2, 2, 3)), dma((2, 2, 3)),
        dma((14,)), dma((14,)),
        dma((2,)), dma((2,)),
        dma((X, 3)), dma((X, 3)),
        dma((Y, 3)), dma((Y, 3)),
        dma((2,)), dma((2,)),
        dma((2, H2, HL)), dma((2, H2, HL)),
    ]
    return pl.pallas_call(
        functools.partial(kernel, X, Y, Z),
        out_shape=jax.ShapeDtypeStruct((TOK, 4 * COLS), BF),
        in_specs=[anyspace] * 7,
        out_specs=anyspace,
        scratch_shapes=scratch,
        cost_estimate=pl.CostEstimate(flops=5_000_000_000, bytes_accessed=4_000_000, transcendentals=1_000_000),
        compiler_params=pltpu.CompilerParams(
            collective_id=0, has_side_effects=True, vmem_limit_bytes=61 * 1024 * 1024
        ),
    )(queries, keys, values, log_decay, level_pick, level_table, out_weight)


def solution(mesh):
    nctx, Z = mesh.shape["ctx"], mesh.shape["head"]
    chips = nctx // 2
    X = 1 << int(math.log2(chips)) // 2
    Y = chips // X
    in_specs = (
        P("ctx", "head"),
        P("ctx", "head"),
        P("ctx", "head"),
        P("head", "ctx"),
        P("head", "ctx"),
        P("head", None, None),
        P("head", "ctx"),
    )
    return jax.shard_map(
        functools.partial(local, X, Y, Z), mesh=mesh, in_specs=in_specs, out_specs=P("ctx", "head"), check_vma=False
    )
```

time: 97.6 us -> 72.3 us (0.74)
  the two profiles are of different devices: /device:TPU:103 before, /device:TPU:1 now
where the time goes in v2:
time: 72.3 us; the launch traced here: 72.2 us
  Pallas kernels  69.9 us (97%)
  local copies, waits for them, and re-layouts  2.26 us (3%)
    pallas_call x1, Pallas kernels, local(): pl.pallas_call(functools.partial(kernel, X, Y, Z), out_shape=jax.ShapeDty...  69.9 us
    unnamed x1, local copies, waits for them, and re-layouts  2.26 us

profile of v2, /device:TPU:1, one launch (start us, length us, event | category | flops | bytes accessed | tf_op | source)
XLA Modules:
  0.0 72.2 jit_solution(9005826805970221208)
XLA Ops:
  0.0 69.9 %shard_map.73 = bf16[512,1024]{1,0:T(8,128)(2,1)} custom-call(bf16[512,512]{1,0:T(8,128)(2,1)} %q_ref.1, bf16[512,512]{1,0:T(8,128)(2,1)} %k_ref.1, bf16[512,512]{1,0:T(8,128)(2,1)} %v_ref.1, f32[4,512]{1,0:T(4,128)} %ld_hbm.1, s32[4,512]{1,0:T(4,128)} %pick_hbm.1, f32[4,8,16]{2,1,0:T(8,128)} %table_hbm.1, bf16[512,256]{1,0:T(8,128)(2,1)} %w_ref.1), custom_call_target="tpu_custom_call" | custom-call | flops 5000000000 | bytes 4000000 | tf_op jit(solution)/shard_map/pallas_call | solution.py:548
  70.0 2.3 %copy.9 = bf16[512,1024]{1,0:T(8,128)(2,1)} copy(bf16[512,1024]{1,0:T(8,128)(2,1)} %shard_map.73) | data formatting | bytes 2097152

commit v3 on v2

--- a/solution.py
+++ b/solution.py
@@ -24,14 +24,15 @@
     X, Y, Z,
     q_ref, k_ref, v_ref, ld_hbm, pick_hbm, table_hbm, w_ref, out_ref,
     ld_ref, pick_ref, table_ref,
-    qb, kb, vb, picks, wrows, bdrows, col, mix, lst, stage, t0, t0p, d0, d0p, fall, xb, xd, yb, yd, rs, rb, ab, wb, acc, ob,
-    in_sem, out_sem, wqs, wqr, w0s, w0r, w1s, w1r, w2s, w2r, wcs, wcr, cs, cr, xs, xr, ys, yr, rss, rsr, rings, ringr,
+    qb, kb, vb, picks, wrows, bdrows, col, kcol, mix, lst, stage, t0, t0p, d0, d0p, fall, xb, xd, yb, yd, rs, rb, ab, wb, acc, ob,
+    in_sem, out_sem, wqs, wqr, w0s, w0r, w1s, w1r, w2s, w2r, wcs, wcr, cs, cr, xs, xr, ys, yr, rss, rsr, rings, ringr, relay_sem,
 ):
     R = X * Y
     RP = TOK // R
     xbits = X.bit_length() - 1
     ybits = Y.bit_length() - 1
     NR = 1 + xbits + ybits
+    H2 = Z // 2
     me = lax.axis_index("ctx")
     z = lax.axis_index("head")
     c = lax.rem(me, 2)
@@ -67,9 +68,6 @@
     greet(me, right)
     greet(me, left)
 
-    for n in range(2):
-        for head in range(Z):
-            greet((y * X + 2 * lax.rem(z, 2) + n) * 2 + c, head)
 
     small = [
         pltpu.make_async_copy(src, dst, in_sem.at[3, n])
@@ -98,7 +96,106 @@
         step *= 2
     wrows[...] = run
     bdrows[...] = jnp.broadcast_to(run[:, BLOCK - 1:BLOCK], run.shape)
+    scale = jnp.exp(bdrows[...] - run)
+    kcol[...] = jnp.concatenate([scale, jnp.zeros((BLOCK - NB * HL, BLOCK), F32)], axis=0).T
     d0[...] = jnp.zeros_like(d0)
+    d0[0:HL, :] = sum(bdrows[b * HL:(b + 1) * HL, :] for b in range(NB))
+
+    for cp in loads[:2 * HL]:
+        cp.wait()
+
+    for h in range(HL):
+        s = []
+        for b in range(NB):
+            kk = kb[h, b * BLOCK:(b + 1) * BLOCK, :].astype(F32)
+            kk = (kk * kcol[:, b * HL + h:b * HL + h + 1]).astype(BF)
+            s.append(lax.dot_general(
+                kk, vb[h, b * BLOCK:(b + 1) * BLOCK, :], (((0,), (0,)), ((), ())), preferred_element_type=F32
+            ))
+        e = [jnp.exp(bdrows[b * HL + h:b * HL + h + 1, :]) for b in range(NB)]
+        pair = e[1] * s[0] + s[1]
+        lst[h, 0] = s[0].astype(BF)
+        lst[h, 1] = pair.astype(BF)
+        lst[h, 2] = s[2].astype(BF)
+        t0[h] = (e[3] * (e[2] * pair + s[2]) + s[3]).astype(BF)
+
+    pl.semaphore_wait(barrier, 1 + (X - 1) + (Y - 1) + 2)
+
+    core_copies = [
+        remote(t0, t0p, cs.at[0], cr.at[0], mate),
+        remote(d0, d0p, cs.at[1], cr.at[1], mate),
+    ]
+    for cp in core_copies:
+        cp.start()
+
+    def relay(turn):
+        if turn > 0:
+            pl.semaphore_wait(relay_sem.at[turn - 1], 2 if turn < H2 else X - 1)
+        if turn < H2 - 1:
+            for head in (left, right):
+                pl.semaphore_signal(relay_sem.at[turn], inc=1, device_id=(me, head), device_id_type=MESH)
+        elif turn == H2 - 1:
+            for s in range(1, X):
+                pl.semaphore_signal(relay_sem.at[turn], inc=1, device_id=(at_x(s), z), device_id_type=MESH)
+
+    relay(0)
+
+    def wq_move(to, start):
+        def both(way):
+            src = w_ref.at[to] if way == 0 else w_ref.at[:, to]
+            if start == 0:
+                return pltpu.make_async_copy(src, stage.at[y], wqr.at[0])
+            return remote(src, stage.at[y], wqs.at[start], wqr.at[start], (at_y(start), z))
+
+        for way in range(2):
+            @pl.when(half == way)
+            def _():
+                both(way).start()
+
+    def wq_done(start):
+        src = lax.rem(y + Y - start, Y)
+        if start == 0:
+            return pltpu.make_async_copy(w_ref.at[0], stage.at[src], wqr.at[0])
+        return remote(w_ref.at[0], stage.at[src], wqs.at[start], wqr.at[start], (at_y(start), z))
+
+    def w0_place(n):
+        row, col_at = lax.rem(n // X + y, Y), lax.rem(n + x, X)
+        plane = 2 * row + x // 2
+        return row, col_at, plane, jnp.logical_and(plane == z, col_at == x)
+
+    def w0_copy(n):
+        row, col_at, plane, _ = w0_place(n)
+        return remote(
+            stage.at[row, col_at],
+            wb.at[y, col_at, c, half, z],
+            w0s.at[n], w0r.at[half, z], ((y * X + col_at) * 2 + c, plane),
+        )
+
+    def w0_send(n, carry):
+        row, col_at, plane, own = w0_place(n)
+
+        @pl.when(own)
+        def _():
+            pltpu.make_async_copy(
+                stage.at[row, col_at],
+                wb.at[y, col_at, c, half, z], w0r.at[half, z],
+            ).start()
+
+        @pl.when(jnp.logical_not(own))
+        def _():
+            w0_copy(n).start()
+
+        return carry
+
+    def w0_pass():
+        wq_done(0).wait()
+        for step in range(1, Y):
+            wq_done(step).wait_recv()
+        lax.fori_loop(0, R, w0_send, 0)
+
+    for step in range(Y):
+        wq_move(lax.rem(y + step, Y), step)
+
     sub = lax.broadcasted_iota(jnp.int32, (8, BLOCK), 0)
 
     def prepare(h, carry):
@@ -116,94 +213,13 @@
             if b == 3:
                 upper = jnp.where(sub == 2, bd[2], upper)
             rows.append(lw * jnp.where(sub == 0, 1.0, jnp.exp(wr + upper)))
-            rows.append(jnp.where(sub == 0, wr, jnp.where(sub == 1, jnp.exp(bd[b] - wr), 0.0)))
+            rows.append(jnp.where(sub == 0, wr, 0.0))
             start = start + bd[b]
         rows.append(jnp.zeros((BLOCK - 16 * NB, BLOCK), F32))
         col[h] = jnp.concatenate(rows, axis=0).T
-        d0[pl.ds(h, 1), :] = start
         return carry
 
     lax.fori_loop(0, HL, prepare, 0)
-
-    for cp in loads[:2 * HL]:
-        cp.wait()
-
-    def states(h, carry):
-        s = []
-        for b in range(NB):
-            kk = kb[h, b * BLOCK:(b + 1) * BLOCK, :].astype(F32)
-            kk = (kk * col[h, :, b * 16 + 9:b * 16 + 10]).astype(BF)
-            s.append(lax.dot_general(
-                kk, vb[h, b * BLOCK:(b + 1) * BLOCK, :], (((0,), (0,)), ((), ())), preferred_element_type=F32
-            ))
-        e = [jnp.exp(bdrows[pl.ds(b * HL + h, 1), :]) for b in range(NB)]
-        pair = e[1] * s[0] + s[1]
-        lst[h, 0] = s[0].astype(BF)
-        lst[h, 1] = pair.astype(BF)
-        lst[h, 2] = s[2].astype(BF)
-        t0[h] = (e[3] * (e[2] * pair + s[2]) + s[3]).astype(BF)
-        return carry
-
-    lax.fori_loop(0, HL, states, 0)
-
-    pl.semaphore_wait(barrier, 1 + (X - 1) + (Y - 1) + 2 + R)
-
-    QR = TOK // Y
-
-    def w_quarter(row):
-        return w_ref.at[pl.ds(pl.multiple_of(row * QR, QR), QR), :]
-
-    wq = [pltpu.make_async_copy(w_quarter(y), stage.at[y], wqr.at[0])]
-    wq_got = [wq[0]]
-    for s in range(1, Y):
-        dev = (at_y(s), z)
-        src = lax.rem(y + Y - s, Y)
-        wq.append(remote(w_quarter(lax.rem(y + s, Y)), stage.at[y], wqs.at[s], wqr.at[s], dev))
-        wq_got.append(remote(w_quarter(y), stage.at[src], wqs.at[s], wqr.at[s], dev))
-    for cp in wq:
-        cp.start()
-
-    def w0_place(n):
-        row, col_at = lax.rem(n // X + y, Y), lax.rem(n + x, X)
-        plane = 2 * row + x // 2
-        return row, col_at, plane, jnp.logical_and(plane == z, col_at == x)
-
-    def w0_copy(n):
-        row, col_at, plane, _ = w0_place(n)
-        return remote(
-            stage.at[row, pl.ds(pl.multiple_of(col_at * RP, RP), RP), :],
-            wb.at[y, col_at, c, half, z],
-            w0s.at[n], w0r.at[half, z], ((y * X + col_at) * 2 + c, plane),
-        )
-
-    def w0_send(n, carry):
-        row, col_at, plane, own = w0_place(n)
-
-        @pl.when(own)
-        def _():
-            pltpu.make_async_copy(
-                stage.at[row, pl.ds(pl.multiple_of(col_at * RP, RP), RP), :],
-                wb.at[y, col_at, c, half, z], w0r.at[half, z],
-            ).start()
-
-        @pl.when(jnp.logical_not(own))
-        def _():
-            w0_copy(n).start()
-
-        return carry
-
-    def w0_pass():
-        wq_got[0].wait()
-        for got in wq_got[1:]:
-            got.wait_recv()
-        lax.fori_loop(0, R, w0_send, 0)
-
-    core_copies = [
-        remote(t0, t0p, cs.at[0], cr.at[0], mate),
-        remote(d0, d0p, cs.at[1], cr.at[1], mate),
-    ]
-    for cp in core_copies:
-        cp.start()
 
     for cp in loads[2 * HL:]:
         cp.wait()
@@ -253,6 +269,7 @@
                 copies.append((cp, remote(theirs, theirs, ssem.at[s - 1, i], rsem.at[s - 1, i], (dev_of(s), z))))
         return copies
 
+    relay(1)
     x_copies = []
     for n in range(2):
         h = 2 * c + n
@@ -264,8 +281,11 @@
     for h in range(HL):
         rb[h, 0] = jnp.where(c == 1, t0p[h].astype(F32), 0.0).astype(BF)
 
+    relay(2)
     inside(0)
+    relay(H2 - 1)
     inside(1)
+    relay(H2)
     w0_pass()
 
     def weighted(buf, dec, n, at, size, before, last):
@@ -320,7 +340,7 @@
 
     def w0_wait(n, carry):
         a, b = n // Z, lax.rem(n, Z)
-        pltpu.make_async_copy(w_ref.at[pl.ds(0, RP), :], wb.at[y, x, c, a, b], w0r.at[a, b]).wait()
+        pltpu.make_async_copy(w_ref.at[0, 0], wb.at[y, x, c, a, b], w0r.at[a, b]).wait()
         return carry
 
     w1 = []
@@ -339,8 +359,6 @@
             cp.start()
             there = wb.at[lax.rem(y + Y - s, Y), x, c, 1]
             w1.append((cp, remote(there, there, w1s.at[1, s - 1], w1r.at[1, s - 1], dev)))
-
-    H2 = Z // 2
 
     def travels(way, d, n):
         return d < H2 - 1 or (n < 2) == (way == 0)
@@ -437,54 +455,67 @@
                     w2_copy(axis, way, 2)
                 across(axis, at, part)
 
-    def project(origins, first, last=False):
-        def tile(u, carry):
-            lhs = jnp.concatenate([ab[origin, h] for origin in origins for h in range(HL)], axis=1)
-            rhs = jnp.concatenate(
-                [wb[:, :, lax.rem(u, 2), u // 2, origin].reshape(TOK, COLS) for origin in origins], axis=0
-            )
-            part = jnp.dot(lhs, rhs, preferred_element_type=F32)
-            if not first:
-                part = part + acc[u]
-            if last:
-                ob[u] = part.astype(BF)
-                out_copy(u).start()
-            else:
-                acc[u] = part
-            return carry
-
-        lax.fori_loop(0, 4, tile, 0)
+    def project(origins, first, last=False, heads=range(HL), shifted=False):
+        for part in range(2):
+            pick = [h if not shifted else lax.rem((y, x)[part] + h, HL) for h in heads]
+
+            def tile(core, carry):
+                u = 2 * part + core
+                lhs = jnp.concatenate([ab[origin, h] for origin in origins for h in pick], axis=1)
+                rhs = jnp.concatenate([
+                    (wb[h, :, core, 0, origin] if part == 0 else wb[:, h, core, 1, origin]).reshape(HD, COLS)
+                    for origin in origins for h in pick
+                ], axis=0)
+                total = jnp.dot(lhs, rhs, preferred_element_type=F32)
+                if not first:
+                    total = total + acc[u]
+                if last:
+                    ob[u] = total.astype(BF)
+                    out_copy(u).start()
+                else:
+                    acc[u] = total
+                return carry
+
+            lax.fori_loop(0, 2, tile, 0)
 
     def out_copy(u):
         return pltpu.make_async_copy(ob.at[u], out_ref.at[:, pl.ds(pl.multiple_of(u * COLS, COLS), COLS)], out_sem.at[u])
 
     waiting = [[z]]
+    behind = []
     begun = False
-    for d in range(H2):
+    for d in range(H2 - 1):
         for n in range(HL):
             for way in range(2):
-                if travels(way, d, n):
-                    ring_got(way, d, n).wait_recv()
-                    if d + 1 < H2 and travels(way, d + 1, n):
-                        ring(way, d + 1, n).start()
+                ring_got(way, d, n).wait_recv()
+                if travels(way, d + 1, n):
+                    ring(way, d + 1, n).start()
             slot = d * HL + n
             if slot == W2_SLOT:
                 w2_pass()
             for k in range(3):
                 if slot == W3_SLOTS[k]:
                     w3_pass(k)
+            if slot == W3_SLOTS[1] + 1:
+                for _, got in wc[:10]:
+                    got.wait_recv()
+            if W3_SLOTS[1] < slot <= W3_SLOTS[2] and waiting:
+                project(waiting[0], not begun, False, (0, 1, 3), True)
+                begun = True
+                behind += waiting.pop(0)
             if slot == W3_SLOTS[2] + 1:
-                for _, got in wc:
+                for _, got in wc[10:]:
                     got.wait_recv()
-            if slot > W3_SLOTS[2] and waiting:
-                project(waiting.pop(0), not begun)
-                begun = True
-        if d + 1 < H2:
-            waiting.append([lax.rem(z + Z - d - 1, Z), lax.rem(z + d + 1, Z)])
+                project(behind, False, False, (2,), True)
+            elif slot > W3_SLOTS[2] and waiting:
+                project(waiting.pop(0), False)
+        waiting.append([lax.rem(z + Z - d - 1, Z), lax.rem(z + d + 1, Z)])
     while waiting:
-        project(waiting.pop(0), not begun)
-        begun = True
-    project([lax.rem(z + H2, Z)], False, True)
+        project(waiting.pop(0), False)
+    for n in range(2):
+        ring_got(0, H2 - 1, n).wait_recv()
+        ring_got(1, H2 - 1, n + 2).wait_recv()
+        project([lax.rem(z + H2, Z)], False, n == 1, (n, n + 2))
 
     def w0_sent(n, carry):
         @pl.when(jnp.logical_not(w0_place(n)[3]))
@@ -494,8 +525,10 @@
         return carry
 
     lax.fori_loop(0, R, w0_sent, 0)
-    for cp in core_copies + wq[1:]:
+    for cp in core_copies:
         cp.wait_send()
+    for step in range(1, Y):
+        wq_done(step).wait_send()
     for n in range(2):
         state_copy(n, 2 * c).wait_send()
     for cp, _ in x_copies[0] + x_copies[1] + y_copies[0] + y_copies[1] + w1 + wc + [(cp, 0) for cp, _, _, _ in w2.values()]:
@@ -521,10 +554,10 @@
         pltpu.VMEM((HL, TOK), F32), pltpu.VMEM((HL, TOK), jnp.int32), pltpu.VMEM(level_table.shape, F32),
         pltpu.VMEM(heads, BF), pltpu.VMEM(heads, BF), pltpu.VMEM(heads, BF),
         pltpu.VMEM((NB * HL, BLOCK), jnp.int32), pltpu.VMEM((NB * HL, BLOCK), F32), pltpu.VMEM((NB * HL, BLOCK), F32),
-        pltpu.VMEM((HL, BLOCK, BLOCK), F32),
+        pltpu.VMEM((HL, BLOCK, BLOCK), F32), pltpu.VMEM((BLOCK, BLOCK), F32),
         pltpu.VMEM(heads, F32),
         pltpu.VMEM((HL, 3) + state, BF),
-        pltpu.VMEM((Y, TOK // Y, COLS), BF),
+        pltpu.VMEM((Y, X, TOK // R, COLS), BF),
         pltpu.VMEM((HL,) + state, BF), pltpu.VMEM((HL,) + state, BF),
         pltpu.VMEM((8, BLOCK), F32), pltpu.VMEM((8, BLOCK), F32), pltpu.VMEM((2, 8, BLOCK), F32),
         pltpu.VMEM((X, 2) + state, BF), pltpu.VMEM((X, 8, BLOCK), F32),
@@ -544,6 +577,7 @@
         dma((Y, 3)), dma((Y, 3)),
         dma((2,)), dma((2,)),
         dma((2, H2, HL)), dma((2, H2, HL)),
+        pltpu.SemaphoreType.REGULAR((H2,)),
     ]
     return pl.pallas_call(
         functools.partial(kernel, X, Y, Z),
@@ -555,7 +589,7 @@
         compiler_params=pltpu.CompilerParams(
             collective_id=0, has_side_effects=True, vmem_limit_bytes=61 * 1024 * 1024
         ),
-    )(queries, keys, values, log_decay, level_pick, level_table, out_weight)
+    )(queries, keys, values, log_decay, level_pick, level_table, out_weight.reshape(Y, X, TOK // R, COLS))
 
 
 def solution(mesh):

time: 72.3 us -> 71 us (0.982)
  Pallas kernels: 69.9 us -> 68.6 us
    pallas_call x1, Pallas kernels: 69.9 us -> 68.6 us  [local(): pl.pallas_call(functools.partial(kernel, X, Y, Z), out_shape=jax.ShapeDty...]
where the time goes in v3:
time: 71 us; the launch traced here: 70.9 us
  Pallas kernels  68.6 us (97%)
  local copies, waits for them, and re-layouts  2.26 us (3%)
    pallas_call x1, Pallas kernels, local(): pl.pallas_call(functools.partial(kernel, X, Y, Z), out_shape=jax.ShapeDty...  68.6 us
    unnamed x1, local copies, waits for them, and re-layouts  2.26 us

profile of v3, /device:TPU:1, one launch (start us, length us, event | category | flops | bytes accessed | tf_op | source)
XLA Modules:
  0.0 70.9 jit_solution(6298957376775358866)
XLA Ops:
  0.0 68.6 %shard_map.73 = bf16[512,1024]{1,0:T(8,128)(2,1)} custom-call(bf16[512,512]{1,0:T(8,128)(2,1)} %q_ref.1, bf16[512,512]{1,0:T(8,128)(2,1)} %k_ref.1, bf16[512,512]{1,0:T(8,128)(2,1)} %v_ref.1, f32[4,512]{1,0:T(4,128)} %ld_hbm.1, s32[4,512]{1,0:T(4,128)} %pick_hbm.1, f32[4,8,16]{2,1,0:T(8,128)} %table_hbm.1, bf16[4,4,32,256]{3,2,1,0:T(8,128)(2,1)} %bitcast.1), custom_call_target="tpu_custom_call" | custom-call | flops 5000000000 | bytes 4000000 | tf_op jit(solution)/shard_map/pallas_call | solution.py:582
  68.6 2.3 %copy.9 = bf16[512,1024]{1,0:T(8,128)(2,1)} copy(bf16[512,1024]{1,0:T(8,128)(2,1)} %shard_map.73) | data formatting | bytes 2097152

commit v4 on v3

--- a/solution.py
+++ b/solution.py
@@ -14,7 +14,7 @@
 TOK = 512
 NB = TOK // BLOCK
 COLS = 256
-W2_SLOT, W3_SLOTS = 2, (5, 7, 9)
+W2_SLOT, W3_SLOTS = 1, (4, 6, 9)
 MESH = pl.DeviceIdType.MESH
 BF = jnp.bfloat16
 F32 = jnp.float32
@@ -65,8 +65,10 @@
         greet(at_x(s), z)
     for s in range(1, Y):
         greet(at_y(s), z)
-    greet(me, right)
-    greet(me, left)
+    for s in range(1, Y):
+        greet((lax.rem(y + s, Y) * X + lax.rem(x + 2, X)) * 2 + c, z)
+    for s in (1, 2, Z - 2, Z - 1):
+        greet(me, lax.rem(z + s, Z))
 
 
     small = [
@@ -119,7 +121,7 @@
         lst[h, 2] = s[2].astype(BF)
         t0[h] = (e[3] * (e[2] * pair + s[2]) + s[3]).astype(BF)
 
-    pl.semaphore_wait(barrier, 1 + (X - 1) + (Y - 1) + 2)
+    pl.semaphore_wait(barrier, 1 + (X - 1) + 2 * (Y - 1) + 4)
 
     core_copies = [
         remote(t0, t0p, cs.at[0], cr.at[0], mate),
@@ -128,56 +130,67 @@
     for cp in core_copies:
         cp.start()
 
+    beside = x + 1 - 2 * lax.rem(x, 2)
+
     def relay(turn):
         if turn > 0:
-            pl.semaphore_wait(relay_sem.at[turn - 1], 2 if turn < H2 else X - 1)
-        if turn < H2 - 1:
-            for head in (left, right):
-                pl.semaphore_signal(relay_sem.at[turn], inc=1, device_id=(me, head), device_id_type=MESH)
-        elif turn == H2 - 1:
-            for s in range(1, X):
-                pl.semaphore_signal(relay_sem.at[turn], inc=1, device_id=(at_x(s), z), device_id_type=MESH)
+            pl.semaphore_wait(relay_sem.at[turn - 1], 4 if turn == 1 else 1)
+        if turn == 0:
+            for s in (1, 2, Z - 2, Z - 1):
+                pl.semaphore_signal(
+                    relay_sem.at[0], inc=1, device_id=(me, lax.rem(z + s, Z)), device_id_type=MESH
+                )
+        elif turn == 1:
+            pl.semaphore_signal(
+                relay_sem.at[1], inc=1, device_id=((y * X + beside) * 2 + c, z), device_id_type=MESH
+            )
 
     relay(0)
 
-    def wq_move(to, start):
-        def both(way):
-            src = w_ref.at[to] if way == 0 else w_ref.at[:, to]
-            if start == 0:
-                return pltpu.make_async_copy(src, stage.at[y], wqr.at[0])
-            return remote(src, stage.at[y], wqs.at[start], wqr.at[start], (at_y(start), z))
-
+    far = lax.rem(x + 2, X)
+
+    def spread_to(other, step):
+        return ((lax.rem(y + step, Y) * X + (far if other else x)) * 2 + c, z)
+
+    def wq_move(other, step):
+        group = 1 - x // 2 if other else x // 2
+        pair, row = pl.ds(2 * group, 2), lax.rem(y + step, Y)
         for way in range(2):
             @pl.when(half == way)
             def _():
-                both(way).start()
-
-    def wq_done(start):
-        src = lax.rem(y + Y - start, Y)
-        if start == 0:
-            return pltpu.make_async_copy(w_ref.at[0], stage.at[src], wqr.at[0])
-        return remote(w_ref.at[0], stage.at[src], wqs.at[start], wqr.at[start], (at_y(start), z))
+                src = w_ref.at[row, pair] if way == 0 else w_ref.at[pair, row]
+                dst = stage.at[x // 2, y]
+                if not other and step == 0:
+                    pltpu.make_async_copy(src, dst, wqr.at[0, 0]).start()
+                else:
+                    remote(src, dst, wqs.at[other, step], wqr.at[other, step], spread_to(other, step)).start()
+
+    def wq_done(other, step):
+        src, dst = w_ref.at[0, pl.ds(0, 2)], stage.at[1 - x // 2 if other else x // 2, lax.rem(y + Y - step, Y)]
+        if not other and step == 0:
+            return pltpu.make_async_copy(src, dst, wqr.at[0, 0])
+        return remote(src, dst, wqs.at[other, step], wqr.at[other, step], spread_to(other, step))
 
     def w0_place(n):
-        row, col_at = lax.rem(n // X + y, Y), lax.rem(n + x, X)
-        plane = 2 * row + x // 2
-        return row, col_at, plane, jnp.logical_and(plane == z, col_at == x)
+        plane, low = lax.rem(n // 2 + z, Z), lax.rem(n + x, 2)
+        col_at = x // 2 * 2 + low
+        return plane, low, col_at, jnp.logical_and(plane == z, col_at == x)
 
     def w0_copy(n):
-        row, col_at, plane, _ = w0_place(n)
+        plane, low, col_at, _ = w0_place(n)
         return remote(
-            stage.at[row, col_at],
+            stage.at[lax.rem(plane, 2), plane // 2, low],
             wb.at[y, col_at, c, half, z],
             w0s.at[n], w0r.at[half, z], ((y * X + col_at) * 2 + c, plane),
         )
 
     def w0_send(n, carry):
-        row, col_at, plane, own = w0_place(n)
+        plane, low, col_at, own = w0_place(n)
 
         @pl.when(own)
         def _():
             pltpu.make_async_copy(
-                stage.at[row, col_at],
+                stage.at[lax.rem(plane, 2), plane // 2, low],
                 wb.at[y, col_at, c, half, z], w0r.at[half, z],
             ).start()
 
@@ -188,38 +201,17 @@
         return carry
 
     def w0_pass():
-        wq_done(0).wait()
-        for step in range(1, Y):
-            wq_done(step).wait_recv()
+        for other in range(2):
+            for step in range(Y):
+                if other + step == 0:
+                    wq_done(0, 0).wait()
+                else:
+                    wq_done(other, step).wait_recv()
         lax.fori_loop(0, R, w0_send, 0)
 
     for step in range(Y):
-        wq_move(lax.rem(y + step, Y), step)
-
-    sub = lax.broadcasted_iota(jnp.int32, (8, BLOCK), 0)
-
-    def prepare(h, carry):
-        tab = table_ref[h]
-        bd = [bdrows[pl.ds(b * HL + h, 1), :] for b in range(NB)]
-        start = jnp.zeros_like(bd[0])
-        rows = []
-        for b in range(NB):
-            pk = jnp.broadcast_to(picks[pl.ds(b * HL + h, 1), :], (8, BLOCK))
-            lw = jnp.zeros((8, BLOCK), F32)
-            for n in range(16):
-                lw = jnp.where(pk == n, tab[:, n:n + 1], lw)
-            wr = wrows[pl.ds(b * HL + h, 1), :]
-            upper = jnp.where(sub >= 3, start, 0.0)
-            if b == 3:
-                upper = jnp.where(sub == 2, bd[2], upper)
-            rows.append(lw * jnp.where(sub == 0, 1.0, jnp.exp(wr + upper)))
-            rows.append(jnp.where(sub == 0, wr, 0.0))
-            start = start + bd[b]
-        rows.append(jnp.zeros((BLOCK - 16 * NB, BLOCK), F32))
-        col[h] = jnp.concatenate(rows, axis=0).T
-        return carry
-
-    lax.fori_loop(0, HL, prepare, 0)
+        wq_move(0, step)
+        wq_move(1, step)
 
     for cp in loads[2 * HL:]:
         cp.wait()
@@ -269,7 +261,6 @@
                 copies.append((cp, remote(theirs, theirs, ssem.at[s - 1, i], rsem.at[s - 1, i], (dev_of(s), z))))
         return copies
 
-    relay(1)
     x_copies = []
     for n in range(2):
         h = 2 * c + n
@@ -278,15 +269,39 @@
         other = t0p[h].astype(F32) * jnp.where(c == 0, 1.0, sec)
         xb[x, n] = (mine + other).astype(BF)
         x_copies.append(spread((xb, xd), x, X, xs, xr, at_x, n))
+    relay(1)
+    sub = lax.broadcasted_iota(jnp.int32, (8, BLOCK), 0)
+
+    def prepare(h, carry):
+        tab = table_ref[h]
+        bd = [bdrows[pl.ds(b * HL + h, 1), :] for b in range(NB)]
+        start = jnp.zeros_like(bd[0])
+        rows = []
+        for b in range(NB):
+            pk = jnp.broadcast_to(picks[pl.ds(b * HL + h, 1), :], (8, BLOCK))
+            lw = jnp.zeros((8, BLOCK), F32)
+            for n in range(16):
+                lw = jnp.where(pk == n, tab[:, n:n + 1], lw)
+            wr = wrows[pl.ds(b * HL + h, 1), :]
+            upper = jnp.where(sub >= 3, start, 0.0)
+            if b == 3:
+                upper = jnp.where(sub == 2, bd[2], upper)
+            rows.append(lw * jnp.where(sub == 0, 1.0, jnp.exp(wr + upper)))
+            rows.append(jnp.where(sub == 0, wr, 0.0))
+            start = start + bd[b]
+        rows.append(jnp.zeros((BLOCK - 16 * NB, BLOCK), F32))
+        col[h] = jnp.concatenate(rows, axis=0).T
+        return carry
+
+    lax.fori_loop(0, HL, prepare, 0)
+
     for h in range(HL):
         rb[h, 0] = jnp.where(c == 1, t0p[h].astype(F32), 0.0).astype(BF)
 
+    inside(0)
     relay(2)
-    inside(0)
-    relay(H2 - 1)
+    w0_pass()
     inside(1)
-    relay(H2)
-    w0_pass()
 
     def weighted(buf, dec, n, at, size, before, last):
         h = 2 * c + n
@@ -527,8 +542,10 @@
     lax.fori_loop(0, R, w0_sent, 0)
     for cp in core_copies:
         cp.wait_send()
-    for step in range(1, Y):
-        wq_done(step).wait_send()
+    for other in range(2):
+        for step in range(Y):
+            if other + step:
+                wq_done(other, step).wait_send()
     for n in range(2):
         state_copy(n, 2 * c).wait_send()
     for cp, _ in x_copies[0] + x_copies[1] + y_copies[0] + y_copies[1] + w1 + wc + [(cp, 0) for cp, _, _, _ in w2.values()]:
@@ -557,7 +574,7 @@
         pltpu.VMEM((HL, BLOCK, BLOCK), F32), pltpu.VMEM((BLOCK, BLOCK), F32),
         pltpu.VMEM(heads, F32),
         pltpu.VMEM((HL, 3) + state, BF),
-        pltpu.VMEM((Y, X, TOK // R, COLS), BF),
+        pltpu.VMEM((2, Y, 2, TOK // R, COLS), BF),
         pltpu.VMEM((HL,) + state, BF), pltpu.VMEM((HL,) + state, BF),
         pltpu.VMEM((8, BLOCK), F32), pltpu.VMEM((8, BLOCK), F32), pltpu.VMEM((2, 8, BLOCK), F32),
         pltpu.VMEM((X, 2) + state, BF), pltpu.VMEM((X, 8, BLOCK), F32),
@@ -567,7 +584,7 @@
         pltpu.VMEM((Y, X, 2, 2, Z, TOK // R, COLS), BF),
         pltpu.VMEM((4, TOK, COLS), F32), pltpu.VMEM((4, TOK, COLS), BF),
         dma((4, HL)), dma((4,)),
-        dma((Y,)), dma((Y,)),
+        dma((2, Y)), dma((2, Y)),
         dma((R,)), dma((2, Z)),
         dma((2, max(X, Y))), dma((2, max(X, Y))),
         dma((2, 2, 3)), dma((2, 2, 3)),
@@ -577,7 +594,7 @@
         dma((Y, 3)), dma((Y, 3)),
         dma((2,)), dma((2,)),
         dma((2, H2, HL)), dma((2, H2, HL)),
-        pltpu.SemaphoreType.REGULAR((H2,)),
+        pltpu.SemaphoreType.REGULAR((2,)),
     ]
     return pl.pallas_call(
         functools.partial(kernel, X, Y, Z),

time: 71 us -> 68.8 us (0.969)
  Pallas kernels: 68.6 us -> 66 us
    pallas_call x1, Pallas kernels: 68.6 us -> 66 us  [local(): pl.pallas_call(functools.partial(kernel, X, Y, Z), out_shape=jax.ShapeDty...]
where the time goes in v4:
time: 68.8 us; the launch traced here: 68.3 us
  Pallas kernels  66 us (96%)
  local copies, waits for them, and re-layouts  2.26 us (3%)
    pallas_call x1, Pallas kernels, local(): pl.pallas_call(functools.partial(kernel, X, Y, Z), out_shape=jax.ShapeDty...  66 us
    unnamed x1, local copies, waits for them, and re-layouts  2.26 us

profile of v4, /device:TPU:1, one launch (start us, length us, event | category | flops | bytes accessed | tf_op | source)
XLA Modules:
  0.0 68.3 jit_solution(1304492404029155179)
XLA Ops:
  0.0 66.0 %shard_map.73 = bf16[512,1024]{1,0:T(8,128)(2,1)} custom-call(bf16[512,512]{1,0:T(8,128)(2,1)} %q_ref.1, bf16[512,512]{1,0:T(8,128)(2,1)} %k_ref.1, bf16[512,512]{1,0:T(8,128)(2,1)} %v_ref.1, f32[4,512]{1,0:T(4,128)} %ld_hbm.1, s32[4,512]{1,0:T(4,128)} %pick_hbm.1, f32[4,8,16]{2,1,0:T(8,128)} %table_hbm.1, bf16[4,4,32,256]{3,2,1,0:T(8,128)(2,1)} %bitcast.1), custom_call_target="tpu_custom_call" | custom-call | flops 5000000000 | bytes 4000000 | tf_op jit(solution)/shard_map/pallas_call | solution.py:599
  66.0 2.3 %copy.9 = bf16[512,1024]{1,0:T(8,128)(2,1)} copy(bf16[512,1024]{1,0:T(8,128)(2,1)} %shard_map.73) | data formatting | bytes 2097152

commit v5 on v4

--- a/solution.py
+++ b/solution.py
@@ -24,8 +24,8 @@
     X, Y, Z,
     q_ref, k_ref, v_ref, ld_hbm, pick_hbm, table_hbm, w_ref, out_ref,
     ld_ref, pick_ref, table_ref,
-    qb, kb, vb, picks, wrows, bdrows, col, kcol, mix, lst, stage, t0, t0p, d0, d0p, fall, xb, xd, yb, yd, rs, rb, ab, wb, acc, ob,
-    in_sem, out_sem, wqs, wqr, w0s, w0r, w1s, w1r, w2s, w2r, wcs, wcr, cs, cr, xs, xr, ys, yr, rss, rsr, rings, ringr, relay_sem,
+    qb, kb, vb, picks, wrows, bdrows, col, kcol, mix, lst, stage, t0, t0p, d0, d0p, fall, xb, xd, yb, yd, rs, rb, ab, wb, acc,
+    in_sem, wqs, wqr, w0s, w0r, w1s, w1r, w2s, w2r, wcs, wcr, cs, cr, xs, xr, ys, yr, rss, rsr, rings, ringr, relay_sem,
 ):
     R = X * Y
     RP = TOK // R
@@ -485,16 +485,12 @@
                 if not first:
                     total = total + acc[u]
                 if last:
-                    ob[u] = total.astype(BF)
-                    out_copy(u).start()
+                    out_ref[:, pl.ds(pl.multiple_of(u * COLS, COLS), COLS)] = total.astype(BF)
                 else:
                     acc[u] = total
                 return carry
 
             lax.fori_loop(0, 2, tile, 0)
-
-    def out_copy(u):
-        return pltpu.make_async_copy(ob.at[u], out_ref.at[:, pl.ds(pl.multiple_of(u * COLS, COLS), COLS)], out_sem.at[u])
 
     waiting = [[z]]
     behind = []
@@ -555,8 +551,6 @@
             for n in range(HL):
                 if travels(way, d, n):
                     ring(way, d, n).wait_send()
-    for u in range(4):
-        out_copy(u).wait()
 
 
 def local(X, Y, Z, queries, keys, values, log_decay, level_pick, level_table, out_weight):
@@ -582,8 +576,8 @@
         pltpu.VMEM((2, NR - 1) + state, BF), pltpu.VMEM((HL, NR) + state, BF),
         pltpu.VMEM((Z,) + heads, BF),
         pltpu.VMEM((Y, X, 2, 2, Z, TOK // R, COLS), BF),
-        pltpu.VMEM((4, TOK, COLS), F32), pltpu.VMEM((4, TOK, COLS), BF),
-        dma((4, HL)), dma((4,)),
+        pltpu.VMEM((4, TOK, COLS), F32),
+        dma((4, HL)),
         dma((2, Y)), dma((2, Y)),
         dma((R,)), dma((2, Z)),
         dma((2, max(X, Y))), dma((2, max(X, Y))),
@@ -596,17 +590,20 @@
         dma((2, H2, HL)), dma((2, H2, HL)),
         pltpu.SemaphoreType.REGULAR((2,)),
     ]
+    operands = (
+        queries, keys, values, log_decay, level_pick, level_table, out_weight.reshape(Y, X, TOK // R, COLS)
+    )
     return pl.pallas_call(
         functools.partial(kernel, X, Y, Z),
         out_shape=jax.ShapeDtypeStruct((TOK, 4 * COLS), BF),
         in_specs=[anyspace] * 7,
-        out_specs=anyspace,
+        out_specs=pl.BlockSpec(memory_space=pltpu.VMEM),
         scratch_shapes=scratch,
         cost_estimate=pl.CostEstimate(flops=5_000_000_000, bytes_accessed=4_000_000, transcendentals=1_000_000),
         compiler_params=pltpu.CompilerParams(
-            collective_id=0, has_side_effects=True, vmem_limit_bytes=61 * 1024 * 1024
+            collective_id=0, has_side_effects=True, vmem_limit_bytes=48 * 1024 * 1024
         ),
-    )(queries, keys, values, log_decay, level_pick, level_table, out_weight.reshape(Y, X, TOK // R, COLS))
+    )(*[pltpu.with_memory_space_constraint(a, pltpu.HBM) for a in operands])
 
 
 def solution(mesh):

time: 68.8 us -> 67.1 us (0.975)
  local copies, waits for them, and re-layouts: 2.26 us -> 0.97 us
    unnamed x1, local copies, waits for them, and re-layouts: 2.26 us -> 0.97 us
where the time goes in v5:
time: 67.1 us; the launch traced here: 66.6 us
  Pallas kernels  65.7 us (98%)
  local copies, waits for them, and re-layouts  0.97 us (1%)
    pallas_call x1, Pallas kernels, local(): pl.pallas_call(functools.partial(kernel, X, Y, Z), out_shape=jax.ShapeDty...  65.7 us

profile of v5, /device:TPU:1, one launch (start us, length us, event | category | flops | bytes accessed | tf_op | source)
XLA Modules:
  0.0 66.6 jit_solution(5418177766536621350)
XLA Ops:
  0.0 65.7 %shard_map.73 = bf16[512,1024]{1,0:T(8,128)(2,1)S(1)} custom-call(bf16[512,512]{1,0:T(8,128)(2,1)} %q_ref.1, bf16[512,512]{1,0:T(8,128)(2,1)} %k_ref.1, bf16[512,512]{1,0:T(8,128)(2,1)} %v_ref.1, f32[4,512]{1,0:T(4,128)} %ld_hbm.1, s32[4,512]{1,0:T(4,128)} %pick_hbm.1, f32[4,8,16]{2,1,0:T(8,128)} %table_hbm.1, bf16[4,4,32,256]{3,2,1,0:T(8,128)(2,1)} %bitcast.1), custom_call_target="tpu_custom_call" | custom-call | flops 5000000000 | bytes 4000000 | tf_op jit(solution)/shard_map/pallas_call | solution.py:596
  65.7 1.0 %copy.9 = bf16[512,1024]{1,0:T(8,128)(2,1)} copy(bf16[512,1024]{1,0:T(8,128)(2,1)S(1)} %shard_map.73) | data formatting | bytes 2097152
